TPU v7x, 32 devices: a whole 2x2x4 slice. The times are simulated.
32 devices in a mesh: seq: 8 (over z, core), table: 4 (over y, x).
Axes of the slice: x: 2, y: 2, z: 4, core: 2. Of those that a mesh axis runs over, the one named last changes fastest.
Arguments:
- columns: bfloat16 [4, 2048, 512], P(None, 'seq', 'table'), may hold values from -6 to 6
- gaps: float32 [4, 2048], P('table', 'seq'), may hold values from 0.2 to 2457.6
- norm_in: float32 [512], replicated, may hold values from 0.1 to 1.9
- w_gate: bfloat16 [512, 1024], replicated, may hold values from -0.25 to 0.25
- w_xbc: bfloat16 [512, 1280], replicated, may hold values from -0.25 to 0.25
- w_step: bfloat16 [512, 16], replicated, may hold values from -0.25 to 0.25
- step_bias: float32 [16], replicated, may hold values from -1 to 1
- conv_weight: float32 [4, 1280], replicated, may hold values from -1 to 1
- conv_bias: float32 [1280], replicated, may hold values from -1.5 to 1.5
- rates: float32 [16], replicated, may hold values from 2.4414063e-05 to 0.04
- norm_out: float32 [1024], replicated, may hold values from 0.1 to 1.9
- w_out: bfloat16 [1024, 512], replicated, may hold values from -0.1875 to 0.1875
Outputs:
- mixed: bfloat16 [4, 2048, 512], P('table', 'seq')
All inputs are finite; a program needn't handle non-finite values.
Results may differ from a plain program's by a relative error of at most 0.02.
Values may be sent and summed in bfloat16 or wider, within the bound.
A program may use at most 64 MiB of HBM per device.

v0:
```python
import jax
import jax.numpy as jnp
from jax import lax
from jax.sharding import PartitionSpec as P

BLOCK = 256


epsilon = 1e-05


def entering(shard, axis, join, neutral):
    place = lax.axis_index(axis)
    gathered = jax.tree.map(
        lambda a, kind: lax.all_gather(a.astype(kind), axis), shard, (jnp.bfloat16, jnp.bfloat16)
    )
    state = jax.tree.map(lambda a, e: jnp.zeros_like(a) + jnp.asarray(e, a.dtype), shard, neutral)

    def one(step, state):
        return join(
            state,
            jax.tree.map(
                lambda a, own: lax.dynamic_index_in_dim(a, step, 0, False).astype(own.dtype),
                gathered,
                shard,
            ),
        )

    return lax.fori_loop(0, place, one, state)


def passed_along(block, axis, distance):
    devices = range(lax.axis_size(axis))
    route = [(i - distance, i) for i in devices if i - distance in devices]
    return lax.ppermute(block, axis, route)


def rms_rows(values, gain):
    return values * lax.rsqrt(jnp.mean(values * values, axis=-1, keepdims=True) + epsilon) * gain


def block_terms(cx, cb, cc, cdt, cda):
    length = cx.shape[0]
    cs = jnp.cumsum(cda, axis=0)
    scores = jnp.dot(cc, cb.T, preferred_element_type=jnp.float32)
    trail = cs.T
    diff = trail[:, :, None] - trail[:, None, :]
    rows = lax.broadcasted_iota(jnp.int32, (length, length), 0)
    cols = lax.broadcasted_iota(jnp.int32, (length, length), 1)
    factor = jnp.exp(jnp.where((rows >= cols)[None], diff, -jnp.inf))
    mix = (scores[None] * factor * cdt.T[:, None, :]).astype(jnp.bfloat16)
    y_in = jnp.einsum("hts,shp->thp", mix, cx, preferred_element_type=jnp.float32)
    weighted = ((jnp.exp(cs[-1][None, :] - cs) * cdt)[:, :, None] * cx.astype(jnp.float32)).astype(
        jnp.bfloat16
    )
    block_state = jnp.einsum("shp,sn->hpn", weighted, cb, preferred_element_type=jnp.float32)
    return (y_in, block_state, cs)


def local_pass(xs, bm, cm, steps_dt, decay):
    length, heads, head_dim = xs.shape
    state_width = bm.shape[1]
    count = length // BLOCK
    blocks = (
        xs.reshape(count, BLOCK, heads, head_dim),
        bm.reshape(count, BLOCK, state_width),
        cm.reshape(count, BLOCK, state_width),
        steps_dt.reshape(count, BLOCK, heads),
        decay.reshape(count, BLOCK, heads),
    )

    def one_block(block):
        return block_terms(block[0], block[1], block[2], block[3], block[4])

    y_in, states, cs = lax.map(one_block, blocks)
    ends = cs[:, -1, :]

    def walk(state, paired):
        return (jnp.exp(paired[0])[:, None, None] * state + paired[1], state)

    final, entries = lax.scan(walk, jnp.zeros(states.shape[1:], jnp.float32), (ends, states))
    starts = jnp.cumsum(ends, axis=0) - ends
    total = jnp.sum(ends, axis=0)
    return (y_in, cs, entries, starts, final, total)


def carried_output(cm, cs, entries, starts, incoming):
    count, length = (cs.shape[0], cs.shape[1])
    queries = cm.reshape(count, length, cm.shape[1])
    enter = (entries + jnp.exp(starts)[:, :, None, None] * incoming[None]).astype(jnp.bfloat16)
    picked = jnp.einsum("ktn,khpn->kthp", queries, enter, preferred_element_type=jnp.float32)
    return jnp.exp(cs)[..., None] * picked


def carry_in(total_part, final_part):

    def combine(earlier, later):
        return (earlier[0] * later[0], later[0][:, :, None, None] * earlier[1] + later[1])

    identity = (jnp.ones_like(total_part), jnp.zeros_like(final_part))
    prefix = entering((jnp.exp(total_part), final_part), "seq", combine, identity)
    return prefix[1]


def local(
    columns,
    gaps,
    norm_in,
    w_gate,
    w_xbc,
    w_step,
    step_bias,
    conv_weight,
    conv_bias,
    rates,
    norm_out,
    w_out,
):
    inner = w_gate.shape[1]
    heads = w_step.shape[1]
    head_dim = inner // heads
    state_width = (w_xbc.shape[1] - inner) // 2
    reach = conv_weight.shape[0] - 1
    normed = rms_rows(
        lax.all_to_all(columns, "table", split_axis=0, concat_axis=2, tiled=True).astype(
            jnp.float32
        ),
        norm_in,
    ).astype(jnp.bfloat16)
    gate = jnp.einsum("brd,de->bre", normed, w_gate, preferred_element_type=jnp.float32).astype(
        jnp.bfloat16
    )
    xbc = jnp.einsum("brd,de->bre", normed, w_xbc, preferred_element_type=jnp.float32).astype(
        jnp.bfloat16
    )
    step_raw = jnp.einsum("brd,de->bre", normed, w_step, preferred_element_type=jnp.float32)
    gate, xbc, step_raw, normed = (gate, xbc, step_raw, normed)
    hists, length = (xbc.shape[0], xbc.shape[1])
    rim = passed_along(xbc[:, length - reach :, :], "seq", 1)
    padded = jnp.concatenate([rim, xbc], axis=1).astype(jnp.float32)
    conv = conv_bias + conv_weight[0] * padded[:, 0:length]
    for offset in range(1, reach + 1):
        conv = conv + conv_weight[offset] * padded[:, offset : offset + length]
    act = jax.nn.silu(conv).astype(jnp.bfloat16)
    xs = act[:, :, :inner].reshape(hists, length, heads, head_dim)
    bm = act[:, :, inner : inner + state_width]
    cm = act[:, :, inner + state_width :]
    steps_dt = jax.nn.softplus(step_raw + step_bias)
    decay = -rates * steps_dt * gaps[:, :, None]
    y_in, cs, entries, starts, final, total = jax.vmap(local_pass)(xs, bm, cm, steps_dt, decay)
    incoming = carry_in(total, final)
    state_terms = jax.vmap(carried_output)(cm, cs, entries, starts, incoming)
    y = (y_in + state_terms).reshape(hists, length, inner)
    gated = y * jax.nn.silu(gate.astype(jnp.float32))
    out_normed = rms_rows(gated, norm_out).astype(jnp.bfloat16)
    return jnp.einsum("bri,id->brd", out_normed, w_out, preferred_element_type=jnp.float32).astype(
        jnp.bfloat16
    )


def solution(mesh):
    in_specs = (
        P(None, "seq", "table"),
        P("table", "seq"),
        P(),
        P(),
        P(),
        P(),
        P(),
        P(),
        P(),
        P(),
        P(),
        P(),
    )
    out_specs = P("table", "seq", None)
    return jax.shard_map(local, mesh=mesh, in_specs=in_specs, out_specs=out_specs, check_vma=False)
```

profile of v0, /device:TPU:25, one launch (start us, length us, event | category | flops | bytes accessed | tf_op | source)
XLA Modules:
  0.0 81.1 jit_solution(2460829700311279722)
XLA Ops:
  6.5 1.9 %copy.33 = bf16[4,256,128]{1,2,0:T(8,128)(2,1)} copy(bf16[4,256,128]{2,1,0:T(8,128)(2,1)} %param.14) | data formatting | bytes 524288 | tf_op args[0]
  8.4 3.4 %all-to-all-start = ((bf16[4,256,128]{1,2,0:T(8,128)(2,1)}), bf16[4,256,128]{1,2,0:T(8,128)(2,1)S(1)}, u32[]{:S(2)}, u32[]{:S(2)}) async-start(bf16[4,256,128]{1,2,0:T(8,128)(2,1)} %copy.33), calls=%async_computation | async-start | bytes 524288 | tf_op jit(solution)/shard_map/all_to_all | solution.py:125
  11.9 0.7 neg.18
  12.6 1.5 %slice_reduce_fusion.5 = (f32[1280]{0:T(1024)}, f32[1280]{0:T(1024)}, f32[1280]{0:T(1024)}, f32[1280]{0:T(1024)}) fusion(f32[4,1280]{1,0:T(4,128)} %param.21), kind=kLoop, calls=%fused_computation.77 | loop fusion | bytes 40960 | tf_op jit(solution)/shard_map/slice | solution.py:141
  14.1 2.0 %all-to-all-done = bf16[4,256,128]{1,2,0:T(8,128)(2,1)S(1)} async-done(((bf16[4,256,128]{1,2,0:T(8,128)(2,1)}), bf16[4,256,128]{1,2,0:T(8,128)(2,1)S(1)}, u32[]{:S(2)}, u32[]{:S(2)}) %all-to-all-start) | async-done | bytes 262176 | tf_op jit(solution)/shard_map/all_to_all | solution.py:125
  16.7 0.6 reduce-window.6
  17.6 0.6 exponential_bitcast_fusion
  18.5 0.5 fusion
  19.1 1.3 %collective-permute-start = (bf16[1,3,1280]{2,1,0:T(4,128)(2,1)S(1)}, bf16[1,3,1280]{2,1,0:T(4,128)(2,1)S(1)}, u32[]{:S(2)}, u32[]{:S(2)}) collective-permute-start(bf16[1,3,1280]{2,1,0:T(4,128)(2,1)S(1)} %slice.65), channel_id=1, source_target_pairs={{0,4},{4,8},{8,12},{12,16},{16,20},{20,24},{24,28},{1,5},{5,9},{9,... | collective-permute-start | bytes 23048 | tf_op jit(solution)/shard_map/ppermute | solution.py:35
  20.4 0.8 exponential_reduce_fusion
  21.3 0.3 copy.40
  21.7 2.1 %collective-permute-done = bf16[1,3,1280]{2,1,0:T(4,128)(2,1)S(1)} collective-permute-done((bf16[1,3,1280]{2,1,0:T(4,128)(2,1)S(1)}, bf16[1,3,1280]{2,1,0:T(4,128)(2,1)S(1)}, u32[]{:S(2)}, u32[]{:S(2)}) %collective-permute-start) | collective-permute-done | bytes 7712 | tf_op jit(solution)/shard_map/ppermute | solution.py:35
  23.8 1.2 %maximum_convert_fusion = f32[1,259,1280]{2,1,0:T(8,128)S(1)} fusion(bf16[1,256,1280]{2,1,0:T(8,128)(2,1)} %copy-done.1, bf16[1,3,1280]{2,1,0:T(4,128)(2,1)S(1)} %collective-permute-done), kind=kLoop, calls=%fused_computation.39 | loop fusion | flops 1326080 | bytes 1989120 | tf_op jit(solution)/shard_map/convert_element_type | solution.py:140
  25.0 0.8 %multiply_convert_fusion.4 = bf16[1,256,1280]{2,1,0:T(8,128)(2,1)S(1)} fusion(f32[1,259,1280]{2,1,0:T(8,128)S(1)} %maximum_convert_fusion, f32[1280]{0:T(1024)S(1)} %copy-done.14, f32[1280]{0:T(1024)S(1)} %copy-done.15, f32[1280]{0:T(1024)S(1)} %copy-done.13, f32[1280]{0:T(1024)S(1)} %copy-done.12, f32[1280]{0:T(1024)S(1)} %copy-done.17), kind=kLoop, calls=%fused_computation.25 | loop fusion | flops 4259840 | bytes 5923840 | tf_op jit(solution)/shard_map/convert_element_type | solution.py:144
  25.9 0.9 %multiply_convert_fusion.6 = bf16[1,256,1024]{2,1,0:T(8,128)(2,1)} fusion(f32[1,256,1024]{2,1,0:T(8,128)S(1)} %copy.40, bf16[1,256,1280]{2,1,0:T(8,128)(2,1)S(1)} %multiply_convert_fusion.4), kind=kLoop, calls=%fused_computation.38 | loop fusion | flops 786432 | bytes 2097152 | tf_op jit(solution)/shard_map/vmap()/while/body/eval_jaxpr/convert_element_type | solution.py:53
  26.8 1.3 %copy.41 = bf16[1,256,1024]{1,2,0:T(8,128)(2,1)S(1)} copy(bf16[1,256,1024]{2,1,0:T(8,128)(2,1)} %multiply_convert_fusion.6) | data formatting | bytes 1048576 | tf_op jit(solution)/shard_map/vmap()/while/body/eval_jaxpr/convert_element_type | solution.py:53
  28.1 1.7 %fusion.14 = bf16[16,64,128]{2,1,0:T(8,128)(2,1)} fusion(bf16[256,16,64]{0,2,1:T(8,128)(2,1)S(1)} %bitcast.113, f32[16]{0:T(128)} %get-tuple-element.112, bf16[1,256,1280]{2,1,0:T(8,128)(2,1)S(1)} %multiply_convert_fusion.4), kind=kOutput, calls=%fused_computation.29 | convolution fusion | flops 67371008 | bytes 852032 | tf_op jit(solution)/shard_map/vmap()/while/body/eval_jaxpr/shp,sn->hpn/dot_general | solution.py:56
  30.0 9.8 %all-gather = bf16[8,1,1,16]{3,2,1,0:T(2,128)(2,1)S(1)} all-gather(bf16[1,1,1,16]{3,2,1,0:T(2,128)(2,1)S(1)} %copy.39), channel_id=2, replica_groups=mesh['seq'=8,'table'=4] {'seq'}, dimensions={0}, use_global_device_ids=true | all-gather | bytes 288 | tf_op jit(solution)/shard_map/all_gather | solution.py:15
  40.3 2.4 %fusion.8 = f32[256,16,64]{0,2,1:T(8,128)} fusion(bf16[256,16,64]{0,2,1:T(8,128)(2,1)S(1)} %bitcast.115, f32[16,256]{1,0:T(8,128)S(1)} %bitcast.116, f32[16,256]{1,0:T(8,128)S(1)} %bitcast_add_fusion, f32[256,256]{1,0:T(8,128)S(1)} %fusion.29, pred[256,256]{1,0:T(8,128)(4,1)S(1)} %iota_compare_fusion), kind=kOutput, calls=%fused_computation.12 | convolution fusion | flops 139460608 | bytes 1933312 | tf_op jit(solution)/shard_map/vmap()/while/body/eval_jaxpr/hts,shp->thp/dot_general | solution.py:52
  42.7 16.9 %all-gather.4.cloned.1.call-done = bf16[128,64,128]{2,1,0:T(8,128)(2,1)} async-done(((bf16[16,64,128]{2,1,0:T(8,128)(2,1)}), bf16[128,64,128]{2,1,0:T(8,128)(2,1)}) %all-gather.4.cloned.1.call-update) | async-done | bytes 2097168 | tf_op jit(solution)/shard_map/all_gather | solution.py:15
  59.7 8.1 %while.3 = (s32[]{:T(128)}, f32[1,16,64,128]{3,2,1,0:T(8,128)S(1)}, s32[]{:T(128)}, bf16[8,1,16]{2,1,0:T(2,128)(2,1)S(1)}, bf16[8,1,16,64,128]{4,3,2,1,0:T(8,128)(2,1)}, /*index=5*/s32[]{:T(128)}, s32[]{:T(128)}, s32[]{:T(128)}) while((s32[]{:T(128)}, f32[1,16,64,128]{3,2,1,0:T(8,128)S(1)}, s32[]{:T(128)}, bf16[8,1,16]{2,1,0:T(2,128)(2,1)S(1)}, ...), condition=%wide.region_4.5_spmd, body=%wide.region_3.4_spmd.sunk | while | flops 393237 | bytes 1311007 | solution.py:29
  59.7 1.1 %convert_add_fusion.2 = f32[1,16,64,128]{3,2,1,0:T(8,128)S(1)} fusion(f32[1,16,64,128]{3,2,1,0:T(8,128)S(1)} %get-tuple-element.168, bf16[8,1,16,64,128]{4,3,2,1,0:T(8,128)(2,1)} %get-tuple-element.179, s32[]{:T(128)S(6)} %select_n.31, f32[16]{0:T(128)S(1)} %bitcast_convert_fusion.2), kind=kLoop, calls=%fused_computation.clone.1 | loop fusion | flops 393216 | bytes 1310788 | tf_op jit(solution)/shard_map/while/body/add | solution.py:98
  60.9 1.1 %convert_add_fusion.2 = f32[1,16,64,128]{3,2,1,0:T(8,128)S(1)} fusion(f32[1,16,64,128]{3,2,1,0:T(8,128)S(1)} %get-tuple-element.168, bf16[8,1,16,64,128]{4,3,2,1,0:T(8,128)(2,1)} %get-tuple-element.179, s32[]{:T(128)S(6)} %select_n.31, f32[16]{0:T(128)S(1)} %bitcast_convert_fusion.2), kind=kLoop, calls=%fused_computation.clone.1 | loop fusion | flops 393216 | bytes 1310788 | tf_op jit(solution)/shard_map/while/body/add | solution.py:98
  62.0 1.1 %convert_add_fusion.2 = f32[1,16,64,128]{3,2,1,0:T(8,128)S(1)} fusion(f32[1,16,64,128]{3,2,1,0:T(8,128)S(1)} %get-tuple-element.168, bf16[8,1,16,64,128]{4,3,2,1,0:T(8,128)(2,1)} %get-tuple-element.179, s32[]{:T(128)S(6)} %select_n.31, f32[16]{0:T(128)S(1)} %bitcast_convert_fusion.2), kind=kLoop, calls=%fused_computation.clone.1 | loop fusion | flops 393216 | bytes 1310788 | tf_op jit(solution)/shard_map/while/body/add | solution.py:98
  63.2 1.1 %convert_add_fusion.2 = f32[1,16,64,128]{3,2,1,0:T(8,128)S(1)} fusion(f32[1,16,64,128]{3,2,1,0:T(8,128)S(1)} %get-tuple-element.168, bf16[8,1,16,64,128]{4,3,2,1,0:T(8,128)(2,1)} %get-tuple-element.179, s32[]{:T(128)S(6)} %select_n.31, f32[16]{0:T(128)S(1)} %bitcast_convert_fusion.2), kind=kLoop, calls=%fused_computation.clone.1 | loop fusion | flops 393216 | bytes 1310788 | tf_op jit(solution)/shard_map/while/body/add | solution.py:98
  64.3 1.1 %convert_add_fusion.2 = f32[1,16,64,128]{3,2,1,0:T(8,128)S(1)} fusion(f32[1,16,64,128]{3,2,1,0:T(8,128)S(1)} %get-tuple-element.168, bf16[8,1,16,64,128]{4,3,2,1,0:T(8,128)(2,1)} %get-tuple-element.179, s32[]{:T(128)S(6)} %select_n.31, f32[16]{0:T(128)S(1)} %bitcast_convert_fusion.2), kind=kLoop, calls=%fused_computation.clone.1 | loop fusion | flops 393216 | bytes 1310788 | tf_op jit(solution)/shard_map/while/body/add | solution.py:98
  65.5 1.1 %convert_add_fusion.2 = f32[1,16,64,128]{3,2,1,0:T(8,128)S(1)} fusion(f32[1,16,64,128]{3,2,1,0:T(8,128)S(1)} %get-tuple-element.168, bf16[8,1,16,64,128]{4,3,2,1,0:T(8,128)(2,1)} %get-tuple-element.179, s32[]{:T(128)S(6)} %select_n.31, f32[16]{0:T(128)S(1)} %bitcast_convert_fusion.2), kind=kLoop, calls=%fused_computation.clone.1 | loop fusion | flops 393216 | bytes 1310788 | tf_op jit(solution)/shard_map/while/body/add | solution.py:98
  66.6 1.1 %convert_add_fusion.2 = f32[1,16,64,128]{3,2,1,0:T(8,128)S(1)} fusion(f32[1,16,64,128]{3,2,1,0:T(8,128)S(1)} %get-tuple-element.168, bf16[8,1,16,64,128]{4,3,2,1,0:T(8,128)(2,1)} %get-tuple-element.179, s32[]{:T(128)S(6)} %select_n.31, f32[16]{0:T(128)S(1)} %bitcast_convert_fusion.2), kind=kLoop, calls=%fused_computation.clone.1 | loop fusion | flops 393216 | bytes 1310788 | tf_op jit(solution)/shard_map/while/body/add | solution.py:98
  67.8 1.6 %fusion.9 = f32[256,16,64]{0,2,1:T(8,128)S(1)} fusion(f32[256,16,64]{0,2,1:T(8,128)} %fusion.8, f32[256,16]{0,1:T(8,128)S(1)} %copy-done.9, f32[1,16,64,128]{3,2,1,0:T(8,128)S(1)} %get-tuple-element.91, f32[16]{0:T(128)} %get-tuple-element.111, bf16[1,256,1280]{2,1,0:T(8,128)(2,1)S(1)} %multiply_convert_fusion.4), kind=kOutput, calls=%fused_computation.14 | convolution fusion | flops 67895296 | bytes 2703424 | tf_op jit(solution)/shard_map/vmap(ktn,khpn->kthp)/dot_general | solution.py:91
  69.4 1.3 %copy.44 = f32[256,1024]{1,0:T(8,128)} copy(f32[256,1024]{0,1:T(8,128)S(1)} %bitcast.111) | data formatting | bytes 2097152 | tf_op jit(solution)/shard_map/reshape | solution.py:153
  70.7 2.3 %multiply_reduce_fusion = (f32[256]{0:T(256)S(1)}, f32[256,1024]{1,0:T(8,128)S(1)}) fusion(f32[256,1024]{1,0:T(8,128)} %copy.44, bf16[256,512]{0,1:T(8,128)(2,1)S(1)} %copy-done.3, bf16[512,1024]{1,0:T(8,128)(2,1)} %param.17), kind=kOutput, calls=%fused_computation.37 | convolution fusion | flops 270794496 | bytes 3408896 | tf_op jit(solution)/shard_map/brd,de->bre/dot_general | solution.py:130
  73.1 1.2 %fusion.15 = bf16[1,256,512]{2,1,0:T(8,128)(2,1)} fusion(bf16[1024,512]{1,0:T(8,128)(2,1)S(1)} %copy-done.4, f32[256,1024]{1,0:T(8,128)S(1)} %get-tuple-element.126, f32[1024]{0:T(1024)S(1)} %copy-done.18, f32[256]{0:T(256)S(1)} %add_rsqrt_fusion), kind=kOutput, calls=%fused_computation.30 | convolution fusion | flops 269352960 | bytes 2364416 | tf_op jit(solution)/shard_map/bri,id->brd/dot_general | solution.py:156
  (79 shorter events, 2.1 us)
Async XLA Ops:
  6.5 12.0 %copy-start = (bf16[512,1280]{1,0:T(8,128)(2,1)S(1)}, bf16[512,1280]{1,0:T(8,128)(2,1)}, u32[]{:S(2)}) copy-start(bf16[512,1280]{1,0:T(8,128)(2,1)} %param.18) | copy-start | bytes 3932164
  6.5 9.7 %copy-start.19 = (f32[512]{0:T(512)S(1)}, f32[512]{0:T(512)}, u32[]{:S(2)}) copy-start(f32[512]{0:T(512)} %param.16) | copy-start | bytes 6148
  6.5 9.8 %copy-start.16 = (bf16[512,16]{0,1:T(8,128)(2,1)S(1)}, bf16[512,16]{0,1:T(8,128)(2,1)}, u32[]{:S(2)}) copy-start(bf16[512,16]{0,1:T(8,128)(2,1)} %param.19) | copy-start | bytes 49156
  6.5 9.8 %copy-start.21 = (f32[16]{0:T(128)S(1)}, f32[16]{0:T(128)}, u32[]{:S(2)}) copy-start(f32[16]{0:T(128)} %param.20) | copy-start | bytes 196
  6.5 10.0 %copy-start.20 = (f32[1,256]{1,0:T(1,128)S(1)}, f32[1,256]{1,0:T(1,128)}, u32[]{:S(2)}) copy-start(f32[1,256]{1,0:T(1,128)} %param.15) | copy-start | bytes 3076
  8.4 7.7 %all-to-all-start = ((bf16[4,256,128]{1,2,0:T(8,128)(2,1)}), bf16[4,256,128]{1,2,0:T(8,128)(2,1)S(1)}, u32[]{:S(2)}, u32[]{:S(2)}) async-start(bf16[4,256,128]{1,2,0:T(8,128)(2,1)} %copy.33), calls=%async_computation | async-start | bytes 524288 | tf_op jit(solution)/shard_map/all_to_all | solution.py:125
  11.9 47.7 %all-gather.4.cloned.1.call-start = ((), (), s32[]{:S(2)}) async-start(), calls=%async_computation.1 | async-start | bytes 2359296 | tf_op jit(solution)/shard_map/all_gather | solution.py:15
  16.4 2.7 %copy-start.2 = (bf16[256,512]{0,1:T(8,128)(2,1)}, bf16[256,512]{0,1:T(8,128)(2,1)S(1)}, u32[]{:S(2)}) copy-start(bf16[256,512]{0,1:T(8,128)(2,1)S(1)} %fusion.21) | copy-start | bytes 786436
  16.6 3.8 %copy-start.5 = (f32[256,16]{0,1:T(8,128)}, f32[256,16]{0,1:T(8,128)S(1)}, u32[]{:S(2)}) copy-start(f32[256,16]{0,1:T(8,128)S(1)} %compare_select_fusion) | copy-start | bytes 49156
  17.6 2.8 %copy-start.7 = (f32[16,2,128]{2,1,0:T(2,128)}, f32[16,2,128]{2,1,0:T(2,128)S(1)}, u32[]{:S(2)}) copy-start(f32[16,2,128]{2,1,0:T(2,128)S(1)} %broadcast.144) | copy-start | bytes 49156
  18.3 2.2 %copy-start.10 = (f32[1,1,256,16]{2,3,1,0:T(8,128)}, f32[1,1,256,16]{2,3,1,0:T(8,128)S(1)}, u32[]{:S(2)}) copy-start(f32[1,1,256,16]{2,3,1,0:T(8,128)S(1)} %fusion.37) | copy-start | bytes 49156
  19.1 2.2 %copy-start.1 = (bf16[1,256,1280]{2,1,0:T(8,128)(2,1)}, bf16[1,256,1280]{2,1,0:T(8,128)(2,1)S(1)}, u32[]{:S(2)}) copy-start(bf16[1,256,1280]{2,1,0:T(8,128)(2,1)S(1)} %fusion) | copy-start | bytes 1966084
  19.1 4.7 %collective-permute-start = (bf16[1,3,1280]{2,1,0:T(4,128)(2,1)S(1)}, bf16[1,3,1280]{2,1,0:T(4,128)(2,1)S(1)}, u32[]{:S(2)}, u32[]{:S(2)}) collective-permute-start(bf16[1,3,1280]{2,1,0:T(4,128)(2,1)S(1)} %slice.65), channel_id=1, source_target_pairs={{0,4},{4,8},{8,12},{12,16},{16,20},{20,24},{24,28},{1,5},{5,9},{9,... | collective-permute-start | bytes 23048 | tf_op jit(solution)/shard_map/ppermute | solution.py:35
  21.6 3.3 %copy-start.12 = (f32[1280]{0:T(1024)S(1)}, f32[1280]{0:T(1024)}, u32[]{:S(2)}) copy-start(f32[1280]{0:T(1024)} %get-tuple-element.107) | copy-start | bytes 15364
  21.7 3.3 %copy-start.13 = (f32[1280]{0:T(1024)S(1)}, f32[1280]{0:T(1024)}, u32[]{:S(2)}) copy-start(f32[1280]{0:T(1024)} %get-tuple-element.108) | copy-start | bytes 15364
  21.7 3.3 %copy-start.14 = (f32[1280]{0:T(1024)S(1)}, f32[1280]{0:T(1024)}, u32[]{:S(2)}) copy-start(f32[1280]{0:T(1024)} %get-tuple-element.109) | copy-start | bytes 15364
  21.7 3.3 %copy-start.15 = (f32[1280]{0:T(1024)S(1)}, f32[1280]{0:T(1024)}, u32[]{:S(2)}) copy-start(f32[1280]{0:T(1024)} %get-tuple-element.110) | copy-start | bytes 15364
  21.7 3.3 %copy-start.17 = (f32[1280]{0:T(1024)S(1)}, f32[1280]{0:T(1024)}, u32[]{:S(2)}) copy-start(f32[1280]{0:T(1024)} %param.22) | copy-start | bytes 15364
  26.8 3.0 %copy-start.11 = (f32[1,1,256,16]{2,3,1,0:T(8,128)S(1)}, f32[1,1,256,16]{2,3,1,0:T(8,128)}, u32[]{:S(2)}) copy-start(f32[1,1,256,16]{2,3,1,0:T(8,128)} %copy-done.10) | copy-start | bytes 49156
  26.8 13.0 %copy-start.8 = (f32[16,2,128]{2,1,0:T(2,128)S(1)}, f32[16,2,128]{2,1,0:T(2,128)}, u32[]{:S(2)}) copy-start(f32[16,2,128]{2,1,0:T(2,128)} %copy-done.7) | copy-start | bytes 49156
  29.8 10.5 %copy-start.6 = (f32[256,16]{0,1:T(8,128)S(1)}, f32[256,16]{0,1:T(8,128)}, u32[]{:S(2)}) copy-start(f32[256,16]{0,1:T(8,128)} %copy-done.5) | copy-start | bytes 49156
  59.6 8.1 %copy-start.9 = (f32[256,16]{0,1:T(8,128)S(1)}, f32[256,16]{0,1:T(8,128)}, u32[]{:S(2)}) copy-start(f32[256,16]{0,1:T(8,128)} %get-tuple-element.123) | copy-start | bytes 49156
  69.4 1.3 %copy-start.3 = (bf16[256,512]{0,1:T(8,128)(2,1)S(1)}, bf16[256,512]{0,1:T(8,128)(2,1)}, u32[]{:S(2)}) copy-start(bf16[256,512]{0,1:T(8,128)(2,1)} %copy-done.2) | copy-start | bytes 786436
  70.7 2.4 %copy-start.4 = (bf16[1024,512]{1,0:T(8,128)(2,1)S(1)}, bf16[1024,512]{1,0:T(8,128)(2,1)}, u32[]{:S(2)}) copy-start(bf16[1024,512]{1,0:T(8,128)(2,1)} %param.25) | copy-start | bytes 3145732
  70.7 2.4 %copy-start.18 = (f32[1024]{0:T(1024)S(1)}, f32[1024]{0:T(1024)}, u32[]{:S(2)}) copy-start(f32[1024]{0:T(1024)} %param.24) | copy-start | bytes 12292
Sparse Core Ops, SparseCore 0:
  29.9 29.6 all-gather.3
where the time goes:
time: 81.7 us; the launch traced here: 81.1 us
  waiting for transfers between devices  21 us (26%)
  other arithmetic  14 us (17%)
  between operations  13.8 us (17%)
  matrix products  10 us (12%)
  blocking collectives  9.84 us (12%)
  local copies, waits for them, and re-layouts  7.47 us (9%)
  starting transfers between devices  4.75 us (6%)
    all_gather x1, waiting for transfers between devices, entering(): lax.all_gather(a.astype(kind), axis)  16.9 us
    all_gather x1, blocking collectives, entering(): lax.all_gather(a.astype(kind), axis)  9.84 us
    add x7, other arithmetic, combine(): later[0][:, :, None, None] * earlier[1] + later[1]  7.78 us
    all_to_all x1, starting transfers between devices, local(): lax.all_to_all(columns, 'table', split_axis=0, concat_axis=2, tiled=True)  3.44 us
    dot_general x1, matrix products, block_terms(): jnp.einsum('hts,shp->thp', mix, cx, preferred_element_type=jnp.float32)  2.38 us
    dot_general x1, matrix products, local(): jnp.einsum('brd,de->bre', normed, w_gate, preferred_element_type=jnp.floa...  2.34 us
    ppermute x1, waiting for transfers between devices, passed_along(): return lax.ppermute(block, axis, route)  2.07 us
    all_to_all x1, waiting for transfers between devices, local(): lax.all_to_all(columns, 'table', split_axis=0, concat_axis=2, tiled=True)  2 us
  transfers between devices with their start and end apart: 3, of which 3 were waited for; matrix products, arithmetic and copies ran while one was open for 8% of the time, Pallas kernels for 0%

commit v1 on v0

v1 whole, which is shorter than its diff:
```python
import functools

import jax
import jax.numpy as jnp
from jax import lax
from jax.experimental import pallas as pl
from jax.experimental.pallas import tpu as pltpu
from jax.sharding import PartitionSpec as P

MESH = pl.DeviceIdType.MESH
epsilon = 1e-05
LOG2E = 1.4426950408889634
HALO = 16
CHUNK = 256
EXTRA = 16


def silu(v):
    half = 0.5 * v
    return half + half * jnp.tanh(half)


def split(v):
    hi = v.astype(jnp.bfloat16)
    return hi, (v - hi.astype(jnp.float32)).astype(jnp.bfloat16)


def dot(a, b):
    return jnp.dot(a, b, preferred_element_type=jnp.float32)


def kernel(
    tables,
    seqs,
    columns,
    gaps_h,
    norm_in_h,
    w_gate_h,
    w_xbc_h,
    w_step_h,
    step_bias_h,
    conv_weight_h,
    conv_bias_h,
    rates_h,
    norm_out_h,
    w_out_h,
    out,
    gaps,
    norm_in,
    w_gate,
    w_xbc,
    w_step,
    step_bias,
    conv_weight,
    conv_bias,
    rates,
    norm_out,
    w_out,
    cols,
    xb,
    xs,
    y_in,
    ecs,
    gate,
    states,
    decays,
    pair_state,
    pair_decay,
    middle,
    entering,
    part_send,
    part_recv,
    chain_send,
    chain_recv,
    share_send,
    load_sem,
    own_sem,
    all_send,
    all_recv,
    halo_send,
    halo_recv,
    psend,
    precv,
    csend,
    crecv,
    ssend,
    srecv,
):
    s = lax.axis_index("seq")
    t = lax.axis_index("table")
    core = lax.rem(s, 2)
    pair = s // 2
    pairs = seqs // 2
    partner = s + 1 - 2 * core
    length = gaps.shape[1]
    inner = w_gate.shape[1]
    heads = rates.shape[0]
    head_dim = inner // heads
    state = (w_xbc.shape[1] - inner) // 2
    taps = conv_weight.shape[0]
    chunks = inner // CHUNK
    half = chunks // 2
    per = CHUNK // head_dim

    sources = (w_xbc_h, w_step_h, norm_in_h, conv_weight_h, conv_bias_h, gaps_h)
    sources += (rates_h, step_bias_h, w_gate_h, norm_out_h, w_out_h)
    places = (w_xbc, w_step, norm_in, conv_weight, conv_bias, gaps)
    places += (rates, step_bias, w_gate, norm_out, w_out)
    loads = [
        pltpu.make_async_copy(a, b, load_sem.at[i])
        for i, (a, b) in enumerate(zip(sources, places))
    ]
    own = pltpu.make_async_copy(columns.at[t], cols.at[t, pl.ds(HALO, length)], own_sem)

    barrier = pltpu.get_barrier_semaphore()

    def greet(where):
        pl.semaphore_signal(barrier, inc=1, device_id=where, device_id_type=MESH)

    for off in range(1, tables):
        greet((s, lax.rem(t + off, tables)))
    greet((partner, t))

    @pl.when(s > 0)
    def _():
        for h in range(tables):
            greet((s - 1, h))

    @pl.when(s < seqs - 1)
    def _():
        for h in range(tables):
            greet((s + 1, h))

    @pl.when(pair > 0)
    def _():
        greet((s - 2, t))

    @pl.when(pair < pairs - 1)
    def _():
        greet((s + 2, t))

    own.start()
    for load in loads:
        load.start()

    @pl.when(s == 0)
    def _():
        for h in range(tables):
            cols[h, 0:HALO, :] = jnp.zeros((HALO, cols.shape[2]), cols.dtype)

    def count(held):
        return jnp.where(held, 1, 0)

    pl.semaphore_wait(
        barrier,
        tables
        + tables * (count(s > 0) + count(s < seqs - 1))
        + count(pair > 0)
        + count(pair < pairs - 1),
    )

    def across(peer, sender):
        return pltpu.make_async_remote_copy(
            src_ref=columns.at[peer],
            dst_ref=cols.at[sender, pl.ds(HALO, length)],
            send_sem=all_send.at[peer],
            recv_sem=all_recv.at[sender],
            device_id=(s, peer),
            device_id_type=MESH,
        )

    def rim(target, peer, sender):
        return pltpu.make_async_remote_copy(
            src_ref=columns.at[peer, pl.ds(length - HALO, HALO)],
            dst_ref=cols.at[sender, pl.ds(0, HALO)],
            send_sem=halo_send.at[peer],
            recv_sem=halo_recv.at[sender],
            device_id=(target, peer),
            device_id_type=MESH,
        )

    peers = [lax.rem(t + off, tables) for off in range(1, tables)]
    for peer in peers:
        across(peer, t).start()

    @pl.when(s < seqs - 1)
    def _():
        for h in range(tables):
            rim(s + 1, h, t).start()

    lane = lax.broadcasted_iota(jnp.int32, (heads, inner), 1) // head_dim
    head = lax.broadcasted_iota(jnp.int32, (heads, inner), 0)
    spread = jnp.where(lane == head, 1.0, 0.0).astype(jnp.bfloat16)
    before = lax.broadcasted_iota(jnp.int32, (length, length), 0)
    after = lax.broadcasted_iota(jnp.int32, (length, length), 1)
    upper = jnp.where(before <= after, 1.0, 0.0).astype(jnp.bfloat16)
    q = length // 2
    keep = lax.broadcasted_iota(jnp.int32, (q, q), 0) >= lax.broadcasted_iota(
        jnp.int32, (q, q), 1
    )
    low = lax.broadcasted_iota(jnp.int32, (length, 2 * head_dim), 1) < head_dim

    def expand(v):
        hi, lo = split(v)
        return dot(hi, spread) + dot(lo, spread)

    for load in loads[:8]:
        load.wait()
    own.wait()
    for peer in peers:
        across(peer, peer).wait_recv()

    @pl.when(s > 0)
    def _():
        for h in range(tables):
            rim(s, h, h).wait_recv()

    u = jnp.concatenate([cols[h] for h in range(tables)], axis=1).astype(jnp.float32)
    scale = lax.rsqrt(jnp.mean(u * u, axis=-1, keepdims=True) + epsilon)
    normed = (u * scale * norm_in[...][None, :]).astype(jnp.bfloat16)
    main = normed[HALO:]

    step_raw = dot(main, w_step[...])
    xb[...] = dot(normed, w_xbc[...]).astype(jnp.bfloat16).astype(jnp.float32)
    raw = step_raw.T + step_bias[...][:, None]
    dt = jnp.maximum(raw, 0.0) + jnp.log1p(jnp.exp(-jnp.abs(raw)))
    da = -rates[...][:, None] * dt * gaps[...]
    d1 = da.astype(jnp.bfloat16)
    left = da - d1.astype(jnp.float32)
    d2, d3 = split(left)
    cs = dot(d1, upper) + (dot(d2, upper) + dot(d3, upper))
    last = cs[:, length - 1 : length]
    ecs[...] = expand(jnp.exp(cs).T)
    weight = expand((jnp.exp(last - cs) * dt).T)
    cs2 = cs * LOG2E
    cs2t = cs2.T
    row2 = jnp.where(dt > 0.0, cs2 - jnp.log(dt) * LOG2E, 3e38)

    def conv(start, width):
        total = conv_bias[start : start + width][None, :]
        for k in range(taps):
            total = total + conv_weight[k : k + 1, start : start + width] * xb[
                pl.ds(HALO - taps + 1 + k, length), start : start + width
            ]
        return silu(total)

    bt = conv(inner, state).T.astype(jnp.bfloat16)
    cm = conv(inner + state, state).astype(jnp.bfloat16)

    for k in range(chunks):
        x = conv(k * CHUNK, CHUNK).astype(jnp.bfloat16)
        xs[k] = x
        cut = slice(k * CHUNK, (k + 1) * CHUNK)
        weighted = (weight[:, cut] * x.astype(jnp.float32)).astype(jnp.bfloat16)
        states[k] = dot(bt, weighted)
        decays[k] = jnp.broadcast_to(ecs[length - 1 : length, cut], (8, CHUNK))

    def to_partner(j):
        return pltpu.make_async_remote_copy(
            src_ref=part_send.at[j],
            dst_ref=part_recv.at[j],
            send_sem=psend.at[j],
            recv_sem=precv.at[j],
            device_id=(partner, t),
            device_id_type=MESH,
        )

    rows = lax.broadcasted_iota(jnp.int32, (EXTRA, CHUNK), 0)
    for j in range(half):
        k = half * (1 - core) + j
        hi, lo = split(decays[k][0:1])
        part_send[j, 0:state, :] = states[k].astype(jnp.bfloat16)
        part_send[j, state : state + EXTRA, :] = jnp.where(
            rows == 0, hi.astype(jnp.float32), jnp.where(rows == 1, lo.astype(jnp.float32), 0.0)
        ).astype(jnp.bfloat16)
        to_partner(j).start()

    scores = dot(cm, bt)
    top = jnp.where(keep, scores[:q, :q], 0.0)
    side = scores[q:, :q]
    end = jnp.where(keep, scores[q:, q:], 0.0)

    def mix_of(h):
        c0, c1 = cs2t[:q, h : h + 1], cs2t[q:, h : h + 1]
        r0, r1 = row2[h : h + 1, :q], row2[h : h + 1, q:]
        m0 = jnp.where(keep, top * jnp.exp2(c0 - r0), 0.0).astype(jnp.bfloat16)
        m1 = (side * jnp.exp2(c1 - r0)).astype(jnp.bfloat16)
        m2 = jnp.where(keep, end * jnp.exp2(c1 - r1), 0.0).astype(jnp.bfloat16)
        return m0, jnp.concatenate([m1, m2], axis=1)

    def intra(k):
        for p in range(per // 2):
            pairx = xs[k, :, p * 2 * head_dim : (p + 1) * 2 * head_dim]
            got = []
            for e in range(2):
                m0, m1 = mix_of(k * per + 2 * p + e)
                got.append(jnp.concatenate([dot(m0, pairx[:q]), dot(m1, pairx)], axis=0))
            y_in[k, :, p * 2 * head_dim : (p + 1) * 2 * head_dim] = jnp.where(low, got[0], got[1])

    def chain(j):
        return pltpu.make_async_remote_copy(
            src_ref=chain_send.at[j],
            dst_ref=chain_recv.at[j],
            send_sem=csend.at[j],
            recv_sem=crecv.at[j],
            device_id=(s + 2, t),
            device_id_type=MESH,
        )

    def share(j, k):
        return pltpu.make_async_remote_copy(
            src_ref=share_send.at[j],
            dst_ref=entering.at[k],
            send_sem=ssend.at[j],
            recv_sem=srecv.at[j],
            device_id=(partner, t),
            device_id_type=MESH,
        )

    odd = core == 1

    def join():
        for j in range(half):
            k = half * core + j
            to_partner(j).wait_recv()
            theirs = part_recv[j, 0:state, :].astype(jnp.float32)
            tail = part_recv[j, state : state + EXTRA, :].astype(jnp.float32)
            their_decay = tail[0:1] + tail[1:2]
            mine = states[k]
            my_decay = decays[k][0:1]
            first = jnp.where(odd, theirs, mine)
            second = jnp.where(odd, mine, theirs)
            first_decay = jnp.where(odd, their_decay, my_decay)
            second_decay = jnp.where(odd, my_decay, their_decay)
            pair_state[j] = second_decay * first + second
            pair_decay[j] = jnp.broadcast_to(second_decay * first_decay, (8, CHUNK))
            middle[j] = first
            decays[k] = jnp.broadcast_to(first_decay, (8, CHUNK))

    def step(entry):
        for j in range(half):
            k = half * core + j
            if entry:
                chain(j).wait_recv()
                came = chain_recv[j].astype(jnp.float32)
                leaving = pair_decay[j][0:1] * came + pair_state[j]
                between = decays[k][0:1] * came + middle[j]
            else:
                came = jnp.zeros((state, CHUNK), jnp.float32)
                leaving = pair_state[j]
                between = middle[j]

            @pl.when(pair < pairs - 1)
            def _():
                chain_send[j] = leaving.astype(jnp.bfloat16)
                chain(j).start()

            share_send[j] = jnp.where(odd, came, between).astype(jnp.bfloat16)
            share(j, k).start()
            entering[k] = jnp.where(odd, between, came).astype(jnp.bfloat16)

    for k in range(chunks):
        intra(k)
        if k == 0:
            join()

            @pl.when(pair == 0)
            def _():
                step(False)

        elif k < chunks - 1:

            @pl.when(pair == k)
            def _():
                step(True)

    loads[8].wait()
    gate[...] = silu(dot(main, w_gate[...]).astype(jnp.bfloat16).astype(jnp.float32))

    @pl.when(pair >= chunks - 1)
    def _():
        step(True)

    for j in range(half):
        share(j, half * (1 - core) + j).wait_recv()
    loads[9].wait()
    loads[10].wait()

    square = jnp.zeros((length, 1), jnp.float32)
    for k in range(chunks):
        cut = slice(k * CHUNK, (k + 1) * CHUNK)
        y = y_in[k] + ecs[:, cut] * dot(cm, entering[k])
        g = y * gate[:, cut]
        square = square + jnp.sum(g * g, axis=-1, keepdims=True)
        y_in[k] = g
    scale = lax.rsqrt(square / inner + epsilon)
    gathered = [
        (y_in[k] * scale * norm_out[k * CHUNK : (k + 1) * CHUNK][None, :]).astype(jnp.bfloat16)
        for k in range(chunks)
    ]
    out[...] = dot(jnp.concatenate(gathered, axis=1), w_out[...]).astype(out.dtype)

    for peer in peers:
        across(peer, t).wait_send()

    @pl.when(s < seqs - 1)
    def _():
        for h in range(tables):
            rim(s + 1, h, t).wait_send()

    for j in range(half):
        to_partner(j).wait_send()
        share(j, half * core + j).wait_send()

    @pl.when(pair < pairs - 1)
    def _():
        for j in range(half):
            chain(j).wait_send()


def local(tables, seqs, *args):
    columns, gaps, norm_in, w_gate, w_xbc, w_step = args[:6]
    step_bias, conv_weight, conv_bias, rates, norm_out, w_out = args[6:]
    length = columns.shape[1]
    inner = w_gate.shape[1]
    state = (w_xbc.shape[1] - inner) // 2
    chunks = inner // CHUNK
    half = chunks // 2
    f32, bf16 = jnp.float32, jnp.bfloat16
    dma = pltpu.SemaphoreType.DMA
    scratch = [pltpu.VMEM(a.shape, a.dtype) for a in args[1:]]
    scratch += [
        pltpu.VMEM((tables, HALO + length, columns.shape[2]), bf16),
        pltpu.VMEM((HALO + length, w_xbc.shape[1]), f32),
        pltpu.VMEM((chunks, length, CHUNK), bf16),
        pltpu.VMEM((chunks, length, CHUNK), f32),
        pltpu.VMEM((length, inner), f32),
        pltpu.VMEM((length, inner), f32),
        pltpu.VMEM((chunks, state, CHUNK), f32),
        pltpu.VMEM((chunks, 8, CHUNK), f32),
        pltpu.VMEM((half, state, CHUNK), f32),
        pltpu.VMEM((half, 8, CHUNK), f32),
        pltpu.VMEM((half, state, CHUNK), f32),
        pltpu.VMEM((chunks, state, CHUNK), bf16),
        pltpu.VMEM((half, state + EXTRA, CHUNK), bf16),
        pltpu.VMEM((half, state + EXTRA, CHUNK), bf16),
        pltpu.VMEM((half, state, CHUNK), bf16),
        pltpu.VMEM((half, state, CHUNK), bf16),
        pltpu.VMEM((half, state, CHUNK), bf16),
        dma((11,)),
        dma(()),
        dma((tables,)),
        dma((tables,)),
        dma((tables,)),
        dma((tables,)),
        dma((half,)),
        dma((half,)),
        dma((half,)),
        dma((half,)),
        dma((half,)),
        dma((half,)),
    ]
    got = pl.pallas_call(
        functools.partial(kernel, tables, seqs),
        out_shape=jax.ShapeDtypeStruct((length, w_out.shape[1]), bf16),
        in_specs=[pl.BlockSpec(memory_space=pl.ANY)] * len(args),
        out_specs=pl.BlockSpec(memory_space=pltpu.VMEM),
        scratch_shapes=scratch,
        compiler_params=pltpu.CompilerParams(
            collective_id=0, has_side_effects=True, vmem_limit_bytes=48 * 2**20
        ),
        cost_estimate=pl.CostEstimate(
            flops=2 * 10**9, bytes_accessed=4 * 10**6, transcendentals=2 * 10**6
        ),
    )(*args)
    return got[None]


def solution(mesh):
    in_specs = (P(None, "seq", "table"), P("table", "seq")) + (P(),) * 10
    return jax.shard_map(
        functools.partial(local, mesh.shape["table"], mesh.shape["seq"]),
        mesh=mesh,
        in_specs=in_specs,
        out_specs=P("table", "seq", None),
        check_vma=False,
    )
```

time: 81.7 us -> 35.1 us (0.43)
  the two profiles are of different devices: /device:TPU:25 before, /device:TPU:29 now
where the time goes in v1:
time: 35.1 us; the launch traced here: 34.6 us
  Pallas kernels  23.5 us (67%)
  local copies, waits for them, and re-layouts  11 us (31%)
    pallas_call x1, Pallas kernels, local(): pl.pallas_call(functools.partial(kernel, tables, seqs), out_shape=jax.Sha...  23.5 us
    unnamed x24, local copies, waits for them, and re-layouts  11 us

profile of v1, /device:TPU:29, one launch (start us, length us, event | category | flops | bytes accessed | tf_op | source)
XLA Modules:
  0.0 34.6 jit_solution(8774445546391731167)
XLA Ops:
  0.0 0.8 %copy.13.w_step_h = bf16[512,16]{1,0:T(8,128)(2,1)S(1)} copy(bf16[512,16]{0,1:T(8,128)(2,1)} %param.17) | data formatting | bytes 32768 | tf_op args[5]
  0.8 0.0 copy-start
  0.9 1.3 %copy-done = bf16[512,1280]{1,0:T(8,128)(2,1)S(1)} copy-done((bf16[512,1280]{1,0:T(8,128)(2,1)S(1)}, bf16[512,1280]{1,0:T(8,128)(2,1)}, u32[]{:S(2)}) %copy-start) | copy-done | bytes 1310744
  2.2 0.0 copy-start.1
  2.2 1.2 %copy-done.1 = bf16[512,1024]{1,0:T(8,128)(2,1)S(1)} copy-done((bf16[512,1024]{1,0:T(8,128)(2,1)S(1)}, bf16[512,1024]{1,0:T(8,128)(2,1)}, u32[]{:S(2)}) %copy-start.1) | copy-done | bytes 1048600
  3.4 0.0 copy-start.2
  3.4 1.2 %copy-done.2 = bf16[1024,512]{1,0:T(8,128)(2,1)S(1)} copy-done((bf16[1024,512]{1,0:T(8,128)(2,1)S(1)}, bf16[1024,512]{1,0:T(8,128)(2,1)}, u32[]{:S(2)}) %copy-start.2) | copy-done | bytes 1048600
  4.6 0.0 copy-start.3
  4.6 0.9 %copy-done.3 = bf16[4,256,128]{2,1,0:T(8,128)(2,1)S(1)} copy-done((bf16[4,256,128]{2,1,0:T(8,128)(2,1)S(1)}, bf16[4,256,128]{2,1,0:T(8,128)(2,1)}, u32[]{:S(2)}) %copy-start.3) | copy-done | bytes 262168
  5.6 0.0 copy-start.4
  5.6 0.7 %copy-done.4 = f32[4,1280]{1,0:T(4,128)S(1)} copy-done((f32[4,1280]{1,0:T(4,128)S(1)}, f32[4,1280]{1,0:T(4,128)}, u32[]{:S(2)}) %copy-start.4) | copy-done | bytes 20504
  6.3 0.0 copy-start.5
  6.3 0.7 %copy-done.5 = f32[1280]{0:T(1024)S(1)} copy-done((f32[1280]{0:T(1024)S(1)}, f32[1280]{0:T(1024)}, u32[]{:S(2)}) %copy-start.5) | copy-done | bytes 5144
  7.0 0.0 copy-start.6
  7.0 0.7 %copy-done.6 = f32[1024]{0:T(1024)S(1)} copy-done((f32[1024]{0:T(1024)S(1)}, f32[1024]{0:T(1024)}, u32[]{:S(2)}) %copy-start.6) | copy-done | bytes 4120
  7.7 0.0 copy-start.7
  7.7 0.7 %copy-done.7 = f32[512]{0:T(512)S(1)} copy-done((f32[512]{0:T(512)S(1)}, f32[512]{0:T(512)}, u32[]{:S(2)}) %copy-start.7) | copy-done | bytes 2072
  8.4 0.0 copy-start.8
  8.4 0.7 %copy-done.8 = f32[1,256]{1,0:T(1,128)S(1)} copy-done((f32[1,256]{1,0:T(1,128)S(1)}, f32[1,256]{1,0:T(1,128)}, u32[]{:S(2)}) %copy-start.8) | copy-done | bytes 1048
  9.0 0.0 copy-start.9
  9.0 0.7 %copy-done.9 = f32[16]{0:T(128)S(1)} copy-done((f32[16]{0:T(128)S(1)}, f32[16]{0:T(128)}, u32[]{:S(2)}) %copy-start.9) | copy-done | bytes 88
  9.7 0.0 copy-start.10
  9.7 0.7 %copy-done.10 = f32[16]{0:T(128)S(1)} copy-done((f32[16]{0:T(128)S(1)}, f32[16]{0:T(128)}, u32[]{:S(2)}) %copy-start.10) | copy-done | bytes 88
  10.3 23.5 %shard_map.118 = bf16[256,512]{1,0:T(8,128)(2,1)S(1)} custom-call(bf16[4,256,128]{2,1,0:T(8,128)(2,1)S(1)} %copy-done.3, f32[1,256]{1,0:T(1,128)S(1)} %copy-done.8, f32[512]{0:T(512)S(1)} %copy-done.7, bf16[512,1024]{1,0:T(8,128)(2,1)S(1)} %copy-done.1, bf16[512,1280]{1,0:T(8,128)(2,1)S(1)} %copy-done, bf16[512,16]{1,0:T(8,128)(2,1)S(1)} %copy.13.w_step_h, ...), custom_call_target="tpu_custom_call" | custom-call | flops 2000000000 | bytes 4000000 | tf_op jit(solution)/shard_map/pallas_call | solution.py:463
  33.9 0.7 %copy.15 = bf16[1,256,512]{2,1,0:T(8,128)(2,1)} copy(bf16[1,256,512]{2,1,0:T(8,128)(2,1)S(1)} %bitcast.1) | data formatting | bytes 524288
Async XLA Ops:
  0.8 1.3 %copy-start = (bf16[512,1280]{1,0:T(8,128)(2,1)S(1)}, bf16[512,1280]{1,0:T(8,128)(2,1)}, u32[]{:S(2)}) copy-start(bf16[512,1280]{1,0:T(8,128)(2,1)} %w_xbc_h.1) | copy-start | bytes 3932164
  2.2 1.2 %copy-start.1 = (bf16[512,1024]{1,0:T(8,128)(2,1)S(1)}, bf16[512,1024]{1,0:T(8,128)(2,1)}, u32[]{:S(2)}) copy-start(bf16[512,1024]{1,0:T(8,128)(2,1)} %w_gate_h.1) | copy-start | bytes 3145732
  3.4 1.2 %copy-start.2 = (bf16[1024,512]{1,0:T(8,128)(2,1)S(1)}, bf16[1024,512]{1,0:T(8,128)(2,1)}, u32[]{:S(2)}) copy-start(bf16[1024,512]{1,0:T(8,128)(2,1)} %w_out_h.1) | copy-start | bytes 3145732
  4.6 0.9 %copy-start.3 = (bf16[4,256,128]{2,1,0:T(8,128)(2,1)S(1)}, bf16[4,256,128]{2,1,0:T(8,128)(2,1)}, u32[]{:S(2)}) copy-start(bf16[4,256,128]{2,1,0:T(8,128)(2,1)} %columns.1) | copy-start | bytes 786436
  5.6 0.7 %copy-start.4 = (f32[4,1280]{1,0:T(4,128)S(1)}, f32[4,1280]{1,0:T(4,128)}, u32[]{:S(2)}) copy-start(f32[4,1280]{1,0:T(4,128)} %conv_weight_h.1) | copy-start | bytes 61444
  6.3 0.7 %copy-start.5 = (f32[1280]{0:T(1024)S(1)}, f32[1280]{0:T(1024)}, u32[]{:S(2)}) copy-start(f32[1280]{0:T(1024)} %conv_bias_h.1) | copy-start | bytes 15364
  7.0 0.7 %copy-start.6 = (f32[1024]{0:T(1024)S(1)}, f32[1024]{0:T(1024)}, u32[]{:S(2)}) copy-start(f32[1024]{0:T(1024)} %norm_out_h.1) | copy-start | bytes 12292
  7.7 0.7 %copy-start.7 = (f32[512]{0:T(512)S(1)}, f32[512]{0:T(512)}, u32[]{:S(2)}) copy-start(f32[512]{0:T(512)} %norm_in_h.1) | copy-start | bytes 6148
  8.4 0.7 %copy-start.8 = (f32[1,256]{1,0:T(1,128)S(1)}, f32[1,256]{1,0:T(1,128)}, u32[]{:S(2)}) copy-start(f32[1,256]{1,0:T(1,128)} %gaps_h.1) | copy-start | bytes 3076
  9.0 0.7 %copy-start.9 = (f32[16]{0:T(128)S(1)}, f32[16]{0:T(128)}, u32[]{:S(2)}) copy-start(f32[16]{0:T(128)} %step_bias_h.1) | copy-start | bytes 196
  9.7 0.7 %copy-start.10 = (f32[16]{0:T(128)S(1)}, f32[16]{0:T(128)}, u32[]{:S(2)}) copy-start(f32[16]{0:T(128)} %rates_h.1) | copy-start | bytes 196

commit v2 on v1

--- a/solution.py
+++ b/solution.py
@@ -12,6 +12,7 @@
 LOG2E = 1.4426950408889634
 HALO = 16
 CHUNK = 256
+PIECE = 128
 EXTRA = 16
 
 
@@ -66,6 +67,7 @@
     decays,
     pair_state,
     pair_decay,
+    first_decays,
     middle,
     entering,
     part_send,
@@ -73,6 +75,9 @@
     chain_send,
     chain_recv,
     share_send,
+    weight,
+    bias_row,
+    out_row,
     load_sem,
     own_sem,
     all_send,
@@ -95,6 +100,7 @@
     length = gaps.shape[1]
     inner = w_gate.shape[1]
     heads = rates.shape[0]
+    pieces = CHUNK // PIECE
     head_dim = inner // heads
     state = (w_xbc.shape[1] - inner) // 2
     taps = conv_weight.shape[0]
@@ -220,9 +226,11 @@
     normed = (u * scale * norm_in[...][None, :]).astype(jnp.bfloat16)
     main = normed[HALO:]
 
-    step_raw = dot(main, w_step[...])
+    step_raw = lax.dot_general(
+        w_step[...], main, (((1,), (1,)), ((), ())), preferred_element_type=jnp.float32
+    )
     xb[...] = dot(normed, w_xbc[...]).astype(jnp.bfloat16).astype(jnp.float32)
-    raw = step_raw.T + step_bias[...][:, None]
+    raw = step_raw + step_bias[...][:, None]
     dt = jnp.maximum(raw, 0.0) + jnp.log1p(jnp.exp(-jnp.abs(raw)))
     da = -rates[...][:, None] * dt * gaps[...]
     d1 = da.astype(jnp.bfloat16)
@@ -230,50 +238,56 @@
     d2, d3 = split(left)
     cs = dot(d1, upper) + (dot(d2, upper) + dot(d3, upper))
     last = cs[:, length - 1 : length]
-    ecs[...] = expand(jnp.exp(cs).T)
-    weight = expand((jnp.exp(last - cs) * dt).T)
+    grown = expand(jnp.exp(cs).T)
+    faded = expand((jnp.exp(last - cs) * dt).T)
+    for k in range(chunks):
+        cut = slice(k * CHUNK, (k + 1) * CHUNK)
+        ecs[k] = grown[:, cut]
+        weight[k] = faded[:, cut]
+        decays[k] = jnp.broadcast_to(grown[length - 1 : length, cut], (8, CHUNK))
+    bias_row[...] = conv_bias[...][None, :]
     cs2 = cs * LOG2E
     cs2t = cs2.T
     row2 = jnp.where(dt > 0.0, cs2 - jnp.log(dt) * LOG2E, 3e38)
 
     def conv(start, width):
-        total = conv_bias[start : start + width][None, :]
+        lanes = pl.ds(start, width)
+        total = bias_row[:, lanes]
         for k in range(taps):
-            total = total + conv_weight[k : k + 1, start : start + width] * xb[
-                pl.ds(HALO - taps + 1 + k, length), start : start + width
+            total = total + conv_weight[pl.ds(k, 1), lanes] * xb[
+                pl.ds(HALO - taps + 1 + k, length), lanes
             ]
         return silu(total)
 
-    bt = conv(inner, state).T.astype(jnp.bfloat16)
-    cm = conv(inner + state, state).astype(jnp.bfloat16)
-
-    for k in range(chunks):
-        x = conv(k * CHUNK, CHUNK).astype(jnp.bfloat16)
-        xs[k] = x
-        cut = slice(k * CHUNK, (k + 1) * CHUNK)
-        weighted = (weight[:, cut] * x.astype(jnp.float32)).astype(jnp.bfloat16)
-        states[k] = dot(bt, weighted)
-        decays[k] = jnp.broadcast_to(ecs[length - 1 : length, cut], (8, CHUNK))
-
-    def to_partner(j):
+    def to_partner(i):
         return pltpu.make_async_remote_copy(
-            src_ref=part_send.at[j],
-            dst_ref=part_recv.at[j],
-            send_sem=psend.at[j],
-            recv_sem=precv.at[j],
+            src_ref=part_send.at[i],
+            dst_ref=part_recv.at[i],
+            send_sem=psend.at[i],
+            recv_sem=precv.at[i],
             device_id=(partner, t),
             device_id_type=MESH,
         )
 
-    rows = lax.broadcasted_iota(jnp.int32, (EXTRA, CHUNK), 0)
-    for j in range(half):
-        k = half * (1 - core) + j
+    rows = lax.broadcasted_iota(jnp.int32, (EXTRA, PIECE), 0)
+    bt = conv(inner, state).T.astype(jnp.bfloat16)
+    cm = conv(inner + state, state).astype(jnp.bfloat16)
+    for j in range(chunks):
+        k = lax.rem(half * (1 - core) + j, chunks)
+        x = conv(pl.multiple_of(k * CHUNK, CHUNK), CHUNK).astype(jnp.bfloat16)
+        xs[k] = x
+        made = dot(bt, (weight[k] * x.astype(jnp.float32)).astype(jnp.bfloat16))
+        if j >= half:
+            states[k] = made
+            continue
         hi, lo = split(decays[k][0:1])
-        part_send[j, 0:state, :] = states[k].astype(jnp.bfloat16)
-        part_send[j, state : state + EXTRA, :] = jnp.where(
-            rows == 0, hi.astype(jnp.float32), jnp.where(rows == 1, lo.astype(jnp.float32), 0.0)
-        ).astype(jnp.bfloat16)
-        to_partner(j).start()
+        hi, lo = hi.astype(jnp.float32), lo.astype(jnp.float32)
+        for e in range(pieces):
+            cut = slice(e * PIECE, (e + 1) * PIECE)
+            tail = jnp.where(rows == 0, hi[:, cut], jnp.where(rows == 1, lo[:, cut], 0.0))
+            part_send[j * pieces + e, 0:state, :] = made[:, cut].astype(jnp.bfloat16)
+            part_send[j * pieces + e, state : state + EXTRA, :] = tail.astype(jnp.bfloat16)
+            to_partner(j * pieces + e).start()
 
     scores = dot(cm, bt)
     top = jnp.where(keep, scores[:q, :q], 0.0)
@@ -297,108 +311,122 @@
                 got.append(jnp.concatenate([dot(m0, pairx[:q]), dot(m1, pairx)], axis=0))
             y_in[k, :, p * 2 * head_dim : (p + 1) * 2 * head_dim] = jnp.where(low, got[0], got[1])
 
-    def chain(j):
+    def chain(i):
         return pltpu.make_async_remote_copy(
-            src_ref=chain_send.at[j],
-            dst_ref=chain_recv.at[j],
-            send_sem=csend.at[j],
-            recv_sem=crecv.at[j],
+            src_ref=chain_send.at[i],
+            dst_ref=chain_recv.at[i],
+            send_sem=csend.at[i],
+            recv_sem=crecv.at[i],
             device_id=(s + 2, t),
             device_id_type=MESH,
         )
 
-    def share(j, k):
+    def share(i, where):
         return pltpu.make_async_remote_copy(
-            src_ref=share_send.at[j],
-            dst_ref=entering.at[k],
-            send_sem=ssend.at[j],
-            recv_sem=srecv.at[j],
+            src_ref=share_send.at[i],
+            dst_ref=entering.at[where * half * pieces + i],
+            send_sem=ssend.at[i],
+            recv_sem=srecv.at[i],
             device_id=(partner, t),
             device_id_type=MESH,
         )
 
     odd = core == 1
 
-    def join():
-        for j in range(half):
-            k = half * core + j
-            to_partner(j).wait_recv()
-            theirs = part_recv[j, 0:state, :].astype(jnp.float32)
-            tail = part_recv[j, state : state + EXTRA, :].astype(jnp.float32)
-            their_decay = tail[0:1] + tail[1:2]
-            mine = states[k]
-            my_decay = decays[k][0:1]
-            first = jnp.where(odd, theirs, mine)
-            second = jnp.where(odd, mine, theirs)
-            first_decay = jnp.where(odd, their_decay, my_decay)
-            second_decay = jnp.where(odd, my_decay, their_decay)
-            pair_state[j] = second_decay * first + second
-            pair_decay[j] = jnp.broadcast_to(second_decay * first_decay, (8, CHUNK))
-            middle[j] = first
-            decays[k] = jnp.broadcast_to(first_decay, (8, CHUNK))
-
-    def step(entry):
-        for j in range(half):
-            k = half * core + j
-            if entry:
-                chain(j).wait_recv()
-                came = chain_recv[j].astype(jnp.float32)
-                leaving = pair_decay[j][0:1] * came + pair_state[j]
-                between = decays[k][0:1] * came + middle[j]
-            else:
-                came = jnp.zeros((state, CHUNK), jnp.float32)
-                leaving = pair_state[j]
-                between = middle[j]
+    def join(i):
+        k, e = half * core + i // pieces, i % pieces
+        cut = slice(e * PIECE, (e + 1) * PIECE)
+        to_partner(i).wait_recv()
+        theirs = part_recv[i, 0:state, :].astype(jnp.float32)
+        tail = part_recv[i, state : state + EXTRA, :].astype(jnp.float32)
+        their_decay = tail[0:1] + tail[1:2]
+        mine = states[k][:, cut]
+        my_decay = decays[k][0:1, cut]
+        first = jnp.where(odd, theirs, mine)
+        second = jnp.where(odd, mine, theirs)
+        first_decay = jnp.where(odd, their_decay, my_decay)
+        second_decay = jnp.where(odd, my_decay, their_decay)
+        total = second_decay * first + second
+
+        @pl.when((pair == 0) & (pairs > 1))
+        def _():
+            chain_send[i] = total.astype(jnp.bfloat16)
+            chain(i).start()
+
+        pair_state[i] = total
+        pair_decay[i] = jnp.broadcast_to(second_decay * first_decay, (8, PIECE))
+        middle[i] = first
+        first_decays[i] = jnp.broadcast_to(first_decay, (8, PIECE))
+
+    def step(i, entry):
+        place = core * half * pieces + i
+        if entry:
+            chain(i).wait_recv()
+            came = chain_recv[i].astype(jnp.float32)
 
             @pl.when(pair < pairs - 1)
             def _():
-                chain_send[j] = leaving.astype(jnp.bfloat16)
-                chain(j).start()
-
-            share_send[j] = jnp.where(odd, came, between).astype(jnp.bfloat16)
-            share(j, k).start()
-            entering[k] = jnp.where(odd, between, came).astype(jnp.bfloat16)
+                leaving = pair_decay[i][0:1] * came + pair_state[i]
+                chain_send[i] = leaving.astype(jnp.bfloat16)
+                chain(i).start()
+
+            between = first_decays[i][0:1] * came + middle[i]
+        else:
+            came = jnp.zeros((state, PIECE), jnp.float32)
+            between = middle[i]
+        share_send[i] = jnp.where(odd, came, between).astype(jnp.bfloat16)
+        share(i, core).start()
+        entering[place] = jnp.where(odd, between, came).astype(jnp.bfloat16)
 
     for k in range(chunks):
         intra(k)
         if k == 0:
-            join()
+            for i in range(half * pieces):
+                join(i)
 
             @pl.when(pair == 0)
             def _():
-                step(False)
+                for i in range(half * pieces):
+                    step(i, False)
 
         elif k < chunks - 1:
 
             @pl.when(pair == k)
             def _():
-                step(True)
+                for i in range(half * pieces):
+                    step(i, True)
 
     loads[8].wait()
-    gate[...] = silu(dot(main, w_gate[...]).astype(jnp.bfloat16).astype(jnp.float32))
-
-    @pl.when(pair >= chunks - 1)
-    def _():
-        step(True)
-
-    for j in range(half):
-        share(j, half * (1 - core) + j).wait_recv()
+    gated = silu(dot(main, w_gate[...]).astype(jnp.bfloat16).astype(jnp.float32))
+    for k in range(chunks):
+        gate[k] = gated[:, k * CHUNK : (k + 1) * CHUNK]
     loads[9].wait()
     loads[10].wait()
+    out_row[...] = norm_out[...][None, :]
+
+    def finish(k, square, total):
+        entry = jnp.concatenate([entering[k * pieces + e] for e in range(pieces)], axis=1)
+        start = pl.multiple_of(k * CHUNK, CHUNK)
+        g = (y_in[k] + ecs[k] * dot(cm, entry)) * gate[k]
+        square = square + jnp.sum(g * g, axis=-1, keepdims=True)
+        scaled = (g * out_row[:, pl.ds(start, CHUNK)]).astype(jnp.bfloat16)
+        return square, total + dot(scaled, w_out[pl.ds(start, CHUNK), :])
 
     square = jnp.zeros((length, 1), jnp.float32)
-    for k in range(chunks):
-        cut = slice(k * CHUNK, (k + 1) * CHUNK)
-        y = y_in[k] + ecs[:, cut] * dot(cm, entering[k])
-        g = y * gate[:, cut]
-        square = square + jnp.sum(g * g, axis=-1, keepdims=True)
-        y_in[k] = g
-    scale = lax.rsqrt(square / inner + epsilon)
-    gathered = [
-        (y_in[k] * scale * norm_out[k * CHUNK : (k + 1) * CHUNK][None, :]).astype(jnp.bfloat16)
-        for k in range(chunks)
-    ]
-    out[...] = dot(jnp.concatenate(gathered, axis=1), w_out[...]).astype(out.dtype)
+    total = jnp.zeros((length, out.shape[1]), jnp.float32)
+    for j in range(half):
+
+        @pl.when(pair >= chunks - 1)
+        def _():
+            for e in range(pieces):
+                step(j * pieces + e, True)
+
+        square, total = finish(half * core + j, square, total)
+    for j in range(half):
+        for e in range(pieces):
+            share(j * pieces + e, 1 - core).wait_recv()
+        square, total = finish(half * (1 - core) + j, square, total)
+    out[...] = (total * lax.rsqrt(square / inner + epsilon)).astype(out.dtype)
 
     for peer in peers:
         across(peer, t).wait_send()
@@ -408,24 +436,25 @@
         for h in range(tables):
             rim(s + 1, h, t).wait_send()
 
-    for j in range(half):
-        to_partner(j).wait_send()
-        share(j, half * core + j).wait_send()
+    for i in range(half * pieces):
+        to_partner(i).wait_send()
+        share(i, core).wait_send()
 
     @pl.when(pair < pairs - 1)
     def _():
-        for j in range(half):
-            chain(j).wait_send()
+        for i in range(half * pieces):
+            chain(i).wait_send()
 
 
 def local(tables, seqs, *args):
+    args = args[:5] + (args[5].T,) + args[6:]
     columns, gaps, norm_in, w_gate, w_xbc, w_step = args[:6]
     step_bias, conv_weight, conv_bias, rates, norm_out, w_out = args[6:]
     length = columns.shape[1]
     inner = w_gate.shape[1]
     state = (w_xbc.shape[1] - inner) // 2
     chunks = inner // CHUNK
-    half = chunks // 2
+    count = chunks // 2 * (CHUNK // PIECE)
     f32, bf16 = jnp.float32, jnp.bfloat16
     dma = pltpu.SemaphoreType.DMA
     scratch = [pltpu.VMEM(a.shape, a.dtype) for a in args[1:]]
@@ -434,40 +463,44 @@
         pltpu.VMEM((HALO + length, w_xbc.shape[1]), f32),
         pltpu.VMEM((chunks, length, CHUNK), bf16),
         pltpu.VMEM((chunks, length, CHUNK), f32),
-        pltpu.VMEM((length, inner), f32),
-        pltpu.VMEM((length, inner), f32),
+        pltpu.VMEM((chunks, length, CHUNK), f32),
+        pltpu.VMEM((chunks, length, CHUNK), f32),
         pltpu.VMEM((chunks, state, CHUNK), f32),
         pltpu.VMEM((chunks, 8, CHUNK), f32),
-        pltpu.VMEM((half, state, CHUNK), f32),
-        pltpu.VMEM((half, 8, CHUNK), f32),
-        pltpu.VMEM((half, state, CHUNK), f32),
-        pltpu.VMEM((chunks, state, CHUNK), bf16),
-        pltpu.VMEM((half, state + EXTRA, CHUNK), bf16),
-        pltpu.VMEM((half, state + EXTRA, CHUNK), bf16),
-        pltpu.VMEM((half, state, CHUNK), bf16),
-        pltpu.VMEM((half, state, CHUNK), bf16),
-        pltpu.VMEM((half, state, CHUNK), bf16),
+        pltpu.VMEM((count, state, PIECE), f32),
+        pltpu.VMEM((count, 8, PIECE), f32),
+        pltpu.VMEM((count, 8, PIECE), f32),
+        pltpu.VMEM((count, state, PIECE), f32),
+        pltpu.VMEM((2 * count, state, PIECE), bf16),
+        pltpu.VMEM((count, state + EXTRA, PIECE), bf16),
+        pltpu.VMEM((count, state + EXTRA, PIECE), bf16),
+        pltpu.VMEM((count, state, PIECE), bf16),
+        pltpu.VMEM((count, state, PIECE), bf16),
+        pltpu.VMEM((count, state, PIECE), bf16),
+        pltpu.VMEM((chunks, length, CHUNK), f32),
+        pltpu.VMEM((1, w_xbc.shape[1]), f32),
+        pltpu.VMEM((1, inner), f32),
         dma((11,)),
         dma(()),
         dma((tables,)),
         dma((tables,)),
         dma((tables,)),
         dma((tables,)),
-        dma((half,)),
-        dma((half,)),
-        dma((half,)),
-        dma((half,)),
-        dma((half,)),
-        dma((half,)),
+        dma((count,)),
+        dma((count,)),
+        dma((count,)),
+        dma((count,)),
+        dma((count,)),
+        dma((count,)),
     ]
     got = pl.pallas_call(
         functools.partial(kernel, tables, seqs),
         out_shape=jax.ShapeDtypeStruct((length, w_out.shape[1]), bf16),
-        in_specs=[pl.BlockSpec(memory_space=pl.ANY)] * len(args),
+        in_specs=[pl.BlockSpec(memory_space=pltpu.HBM)] * len(args),
         out_specs=pl.BlockSpec(memory_space=pltpu.VMEM),
         scratch_shapes=scratch,
         compiler_params=pltpu.CompilerParams(
-            collective_id=0, has_side_effects=True, vmem_limit_bytes=48 * 2**20
+            collective_id=0, has_side_effects=True, vmem_limit_bytes=63 * 2**20
         ),
         cost_estimate=pl.CostEstimate(
             flops=2 * 10**9, bytes_accessed=4 * 10**6, transcendentals=2 * 10**6

time: 35.1 us -> 24.9 us (0.71)
  the two profiles are of different devices: /device:TPU:29 before, /device:TPU:25 now
where the time goes in v2:
time: 24.9 us; the launch traced here: 24.7 us
  Pallas kernels  23.1 us (93%)
  local copies, waits for them, and re-layouts  1.67 us (7%)
    pallas_call x1, Pallas kernels, local(): pl.pallas_call(functools.partial(kernel, tables, seqs), out_shape=jax.Sha...  23.1 us
    unnamed x1, local copies, waits for them, and re-layouts  1.67 us

profile of v2, /device:TPU:25, one launch (start us, length us, event | category | flops | bytes accessed | tf_op | source)
XLA Modules:
  0.0 24.7 jit_solution(16781275197282265595)
XLA Ops:
  0.0 23.1 %shard_map.118 = bf16[256,512]{1,0:T(8,128)(2,1)} custom-call(bf16[4,256,128]{2,1,0:T(8,128)(2,1)} %columns.1, f32[1,256]{1,0:T(1,128)} %gaps_h.1, f32[512]{0:T(512)} %norm_in_h.1, bf16[512,1024]{1,0:T(8,128)(2,1)} %w_gate_h.1, bf16[512,1280]{1,0:T(8,128)(2,1)} %w_xbc_h.1, bf16[16,512]{1,0:T(8,128)(2,1)} %bitcast.3, f32[16]{0:T(128)} %step_bias_h.1, ...), custom_call_target="tpu_custom_call" | custom-call | flops 2000000000 | bytes 4000000 | tf_op jit(solution)/shard_map/pallas_call | solution.py:496
  23.1 1.7 %copy.14 = bf16[1,256,512]{2,1,0:T(8,128)(2,1)} copy(bf16[1,256,512]{2,1,0:T(8,128)(2,1)} %bitcast.2) | data formatting | bytes 524288

commit v3 on v2

--- a/solution.py
+++ b/solution.py
@@ -13,6 +13,7 @@
 HALO = 16
 CHUNK = 256
 PIECE = 128
+ROWS = 64
 EXTRA = 16
 
 
@@ -75,7 +76,8 @@
     chain_send,
     chain_recv,
     share_send,
-    weight,
+    spread_s,
+    nm,
     bias_row,
     out_row,
     load_sem,
@@ -103,6 +105,7 @@
     pieces = CHUNK // PIECE
     head_dim = inner // heads
     state = (w_xbc.shape[1] - inner) // 2
+    parts = state // ROWS
     taps = conv_weight.shape[0]
     chunks = inner // CHUNK
     half = chunks // 2
@@ -165,12 +168,14 @@
         + count(pair < pairs - 1),
     )
 
-    def across(peer, sender):
+    q = length // 2
+
+    def across(r, peer, sender):
         return pltpu.make_async_remote_copy(
-            src_ref=columns.at[peer],
-            dst_ref=cols.at[sender, pl.ds(HALO, length)],
-            send_sem=all_send.at[peer],
-            recv_sem=all_recv.at[sender],
+            src_ref=columns.at[peer, pl.ds(r * q, q)],
+            dst_ref=cols.at[sender, pl.ds(HALO + r * q, q)],
+            send_sem=all_send.at[r, peer],
+            recv_sem=all_recv.at[r, sender],
             device_id=(s, peer),
             device_id_type=MESH,
         )
@@ -187,49 +192,65 @@
 
     peers = [lax.rem(t + off, tables) for off in range(1, tables)]
     for peer in peers:
-        across(peer, t).start()
+        across(0, peer, t).start()
 
     @pl.when(s < seqs - 1)
     def _():
         for h in range(tables):
             rim(s + 1, h, t).start()
 
+    for peer in peers:
+        across(1, peer, t).start()
+
     lane = lax.broadcasted_iota(jnp.int32, (heads, inner), 1) // head_dim
     head = lax.broadcasted_iota(jnp.int32, (heads, inner), 0)
-    spread = jnp.where(lane == head, 1.0, 0.0).astype(jnp.bfloat16)
+    spread_s[...] = jnp.where(lane == head, 1.0, 0.0).astype(jnp.bfloat16)
     before = lax.broadcasted_iota(jnp.int32, (length, length), 0)
     after = lax.broadcasted_iota(jnp.int32, (length, length), 1)
     upper = jnp.where(before <= after, 1.0, 0.0).astype(jnp.bfloat16)
-    q = length // 2
     keep = lax.broadcasted_iota(jnp.int32, (q, q), 0) >= lax.broadcasted_iota(
         jnp.int32, (q, q), 1
     )
     low = lax.broadcasted_iota(jnp.int32, (length, 2 * head_dim), 1) < head_dim
 
-    def expand(v):
+    def expand(v, lanes):
         hi, lo = split(v)
-        return dot(hi, spread) + dot(lo, spread)
+        return dot(hi, spread_s[:, lanes]) + dot(lo, spread_s[:, lanes])
 
     for load in loads[:8]:
         load.wait()
     own.wait()
+    bias_row[...] = conv_bias[...][None, :]
+
+    def norm(begin, end):
+        u = jnp.concatenate([cols[h, begin:end, :] for h in range(tables)], axis=1)
+        u = u.astype(jnp.float32)
+        scale = lax.rsqrt(jnp.mean(u * u, axis=-1, keepdims=True) + epsilon)
+        nm[begin:end, :] = (u * scale * norm_in[...][None, :]).astype(jnp.bfloat16)
+
+    def project(begin, end, lanes):
+        made = dot(nm[begin:end, :], w_xbc[:, lanes])
+        xb[begin:end, lanes] = made.astype(jnp.bfloat16).astype(jnp.float32)
+
     for peer in peers:
-        across(peer, peer).wait_recv()
+        across(0, peer, peer).wait_recv()
 
     @pl.when(s > 0)
     def _():
         for h in range(tables):
             rim(s, h, h).wait_recv()
 
-    u = jnp.concatenate([cols[h] for h in range(tables)], axis=1).astype(jnp.float32)
-    scale = lax.rsqrt(jnp.mean(u * u, axis=-1, keepdims=True) + epsilon)
-    normed = (u * scale * norm_in[...][None, :]).astype(jnp.bfloat16)
-    main = normed[HALO:]
-
+    norm(0, HALO + q)
+    project(0, HALO + q, slice(None))
+    for peer in peers:
+        across(1, peer, peer).wait_recv()
+    norm(HALO + q, HALO + length)
+
+    main = nm[HALO:, :]
     step_raw = lax.dot_general(
         w_step[...], main, (((1,), (1,)), ((), ())), preferred_element_type=jnp.float32
     )
-    xb[...] = dot(normed, w_xbc[...]).astype(jnp.bfloat16).astype(jnp.float32)
+    project(HALO + q, HALO + length, slice(inner, inner + 2 * state))
     raw = step_raw + step_bias[...][:, None]
     dt = jnp.maximum(raw, 0.0) + jnp.log1p(jnp.exp(-jnp.abs(raw)))
     da = -rates[...][:, None] * dt * gaps[...]
@@ -238,17 +259,9 @@
     d2, d3 = split(left)
     cs = dot(d1, upper) + (dot(d2, upper) + dot(d3, upper))
     last = cs[:, length - 1 : length]
-    grown = expand(jnp.exp(cs).T)
-    faded = expand((jnp.exp(last - cs) * dt).T)
-    for k in range(chunks):
-        cut = slice(k * CHUNK, (k + 1) * CHUNK)
-        ecs[k] = grown[:, cut]
-        weight[k] = faded[:, cut]
-        decays[k] = jnp.broadcast_to(grown[length - 1 : length, cut], (8, CHUNK))
-    bias_row[...] = conv_bias[...][None, :]
-    cs2 = cs * LOG2E
-    cs2t = cs2.T
-    row2 = jnp.where(dt > 0.0, cs2 - jnp.log(dt) * LOG2E, 3e38)
+    cst = cs.T
+    faded = (jnp.exp(last - cs) * dt).T
+    closing = jnp.exp(cst[length - 16 :])
 
     def conv(start, width):
         lanes = pl.ds(start, width)
@@ -271,12 +284,16 @@
 
     rows = lax.broadcasted_iota(jnp.int32, (EXTRA, PIECE), 0)
     bt = conv(inner, state).T.astype(jnp.bfloat16)
-    cm = conv(inner + state, state).astype(jnp.bfloat16)
     for j in range(chunks):
         k = lax.rem(half * (1 - core) + j, chunks)
-        x = conv(pl.multiple_of(k * CHUNK, CHUNK), CHUNK).astype(jnp.bfloat16)
+        start = pl.multiple_of(k * CHUNK, CHUNK)
+        lanes = pl.ds(start, CHUNK)
+        project(HALO + q, HALO + length, lanes)
+        x = conv(start, CHUNK).astype(jnp.bfloat16)
         xs[k] = x
-        made = dot(bt, (weight[k] * x.astype(jnp.float32)).astype(jnp.bfloat16))
+        weighted = expand(faded, lanes) * x.astype(jnp.float32)
+        made = dot(bt, weighted.astype(jnp.bfloat16))
+        decays[k] = jnp.broadcast_to(expand(closing, lanes)[15:16], (8, CHUNK))
         if j >= half:
             states[k] = made
             continue
@@ -289,34 +306,12 @@
             part_send[j * pieces + e, state : state + EXTRA, :] = tail.astype(jnp.bfloat16)
             to_partner(j * pieces + e).start()
 
-    scores = dot(cm, bt)
-    top = jnp.where(keep, scores[:q, :q], 0.0)
-    side = scores[q:, :q]
-    end = jnp.where(keep, scores[q:, q:], 0.0)
-
-    def mix_of(h):
-        c0, c1 = cs2t[:q, h : h + 1], cs2t[q:, h : h + 1]
-        r0, r1 = row2[h : h + 1, :q], row2[h : h + 1, q:]
-        m0 = jnp.where(keep, top * jnp.exp2(c0 - r0), 0.0).astype(jnp.bfloat16)
-        m1 = (side * jnp.exp2(c1 - r0)).astype(jnp.bfloat16)
-        m2 = jnp.where(keep, end * jnp.exp2(c1 - r1), 0.0).astype(jnp.bfloat16)
-        return m0, jnp.concatenate([m1, m2], axis=1)
-
-    def intra(k):
-        for p in range(per // 2):
-            pairx = xs[k, :, p * 2 * head_dim : (p + 1) * 2 * head_dim]
-            got = []
-            for e in range(2):
-                m0, m1 = mix_of(k * per + 2 * p + e)
-                got.append(jnp.concatenate([dot(m0, pairx[:q]), dot(m1, pairx)], axis=0))
-            y_in[k, :, p * 2 * head_dim : (p + 1) * 2 * head_dim] = jnp.where(low, got[0], got[1])
-
-    def chain(i):
+    def chain(i, r):
         return pltpu.make_async_remote_copy(
-            src_ref=chain_send.at[i],
-            dst_ref=chain_recv.at[i],
-            send_sem=csend.at[i],
-            recv_sem=crecv.at[i],
+            src_ref=chain_send.at[i, pl.ds(r * ROWS, ROWS)],
+            dst_ref=chain_recv.at[i, pl.ds(r * ROWS, ROWS)],
+            send_sem=csend.at[i, r],
+            recv_sem=crecv.at[i, r],
             device_id=(s + 2, t),
             device_id_type=MESH,
         )
@@ -351,7 +346,8 @@
         @pl.when((pair == 0) & (pairs > 1))
         def _():
             chain_send[i] = total.astype(jnp.bfloat16)
-            chain(i).start()
+            for r in range(parts):
+                chain(i, r).start()
 
         pair_state[i] = total
         pair_decay[i] = jnp.broadcast_to(second_decay * first_decay, (8, PIECE))
@@ -361,43 +357,84 @@
     def step(i, entry):
         place = core * half * pieces + i
         if entry:
-            chain(i).wait_recv()
-            came = chain_recv[i].astype(jnp.float32)
-
-            @pl.when(pair < pairs - 1)
-            def _():
-                leaving = pair_decay[i][0:1] * came + pair_state[i]
-                chain_send[i] = leaving.astype(jnp.bfloat16)
-                chain(i).start()
-
-            between = first_decays[i][0:1] * came + middle[i]
+            for r in range(parts):
+                band = slice(r * ROWS, (r + 1) * ROWS)
+                chain(i, r).wait_recv()
+                came = chain_recv[i, band, :].astype(jnp.float32)
+
+                @pl.when(pair < pairs - 1)
+                def _():
+                    leaving = pair_decay[i][0:1] * came + pair_state[i, band, :]
+                    chain_send[i, band, :] = leaving.astype(jnp.bfloat16)
+                    chain(i, r).start()
+
+                between = first_decays[i][0:1] * came + middle[i, band, :]
+                share_send[i, band, :] = jnp.where(odd, came, between).astype(jnp.bfloat16)
+                entering[place, band, :] = jnp.where(odd, between, came).astype(jnp.bfloat16)
         else:
             came = jnp.zeros((state, PIECE), jnp.float32)
             between = middle[i]
-        share_send[i] = jnp.where(odd, came, between).astype(jnp.bfloat16)
+            share_send[i] = jnp.where(odd, came, between).astype(jnp.bfloat16)
+            entering[place] = jnp.where(odd, between, came).astype(jnp.bfloat16)
         share(i, core).start()
-        entering[place] = jnp.where(odd, between, came).astype(jnp.bfloat16)
+
+    @pl.when(pair == 0)
+    def _():
+        for i in range(half * pieces):
+            join(i)
+
+    cm = conv(inner + state, state).astype(jnp.bfloat16)
+    cs2 = cs * LOG2E
+    cs2t = cst * LOG2E
+    row2 = jnp.where(dt > 0.0, cs2 - jnp.log(dt) * LOG2E, 3e38)
+    scores = dot(cm, bt)
+    top = jnp.where(keep, scores[:q, :q], 0.0)
+    side = scores[q:, :q]
+    end = jnp.where(keep, scores[q:, q:], 0.0)
+
+    def mix_of(h):
+        c0, c1 = cs2t[:q, h : h + 1], cs2t[q:, h : h + 1]
+        r0, r1 = row2[h : h + 1, :q], row2[h : h + 1, q:]
+        m0 = jnp.where(keep, top * jnp.exp2(c0 - r0), 0.0).astype(jnp.bfloat16)
+        m1 = (side * jnp.exp2(c1 - r0)).astype(jnp.bfloat16)
+        m2 = jnp.where(keep, end * jnp.exp2(c1 - r1), 0.0).astype(jnp.bfloat16)
+        return m0, jnp.concatenate([m1, m2], axis=1)
+
+    def intra(k):
+        for p in range(per // 2):
+            pairx = xs[k, :, p * 2 * head_dim : (p + 1) * 2 * head_dim]
+            got = []
+            for e in range(2):
+                m0, m1 = mix_of(k * per + 2 * p + e)
+                got.append(jnp.concatenate([dot(m0, pairx[:q]), dot(m1, pairx)], axis=0))
+            y_in[k, :, p * 2 * head_dim : (p + 1) * 2 * head_dim] = jnp.where(low, got[0], got[1])
 
     for k in range(chunks):
         intra(k)
         if k == 0:
-            for i in range(half * pieces):
-                join(i)
+
+            @pl.when(pair > 0)
+            def _():
+                for i in range(half * pieces):
+                    join(i)
 
             @pl.when(pair == 0)
             def _():
                 for i in range(half * pieces):
                     step(i, False)
 
-        elif k < chunks - 1:
-
-            @pl.when(pair == k)
+        if k != 1 and k < chunks - 1:
+
+            @pl.when(pair == max(k, 1))
             def _():
                 for i in range(half * pieces):
                     step(i, True)
 
+    grown = expand(jnp.exp(cst), slice(None))
+    for k in range(chunks):
+        ecs[k] = grown[:, k * CHUNK : (k + 1) * CHUNK]
     loads[8].wait()
-    gated = silu(dot(main, w_gate[...]).astype(jnp.bfloat16).astype(jnp.float32))
+    gated = silu(dot(nm[HALO:, :], w_gate[...]).astype(jnp.bfloat16).astype(jnp.float32))
     for k in range(chunks):
         gate[k] = gated[:, k * CHUNK : (k + 1) * CHUNK]
     loads[9].wait()
@@ -429,7 +466,8 @@
     out[...] = (total * lax.rsqrt(square / inner + epsilon)).astype(out.dtype)
 
     for peer in peers:
-        across(peer, t).wait_send()
+        for r in range(2):
+            across(r, peer, t).wait_send()
 
     @pl.when(s < seqs - 1)
     def _():
@@ -443,7 +481,22 @@
     @pl.when(pair < pairs - 1)
     def _():
         for i in range(half * pieces):
-            chain(i).wait_send()
+            for r in range(parts):
+                chain(i, r).wait_send()
+
+
+def move(got, out, sem):
+    size = got.shape[0] // 4
+    copies = [
+        pltpu.make_async_copy(
+            got.at[pl.ds(i * size, size)], out.at[0, pl.ds(i * size, size)], sem.at[i]
+        )
+        for i in range(4)
+    ]
+    for copy in copies:
+        copy.start()
+    for copy in copies:
+        copy.wait()
 
 
 def local(tables, seqs, *args):
@@ -477,19 +530,20 @@
         pltpu.VMEM((count, state, PIECE), bf16),
         pltpu.VMEM((count, state, PIECE), bf16),
         pltpu.VMEM((count, state, PIECE), bf16),
-        pltpu.VMEM((chunks, length, CHUNK), f32),
+        pltpu.VMEM((rates.shape[0], inner), bf16),
+        pltpu.VMEM((HALO + length, w_gate.shape[0]), bf16),
         pltpu.VMEM((1, w_xbc.shape[1]), f32),
         pltpu.VMEM((1, inner), f32),
         dma((11,)),
         dma(()),
-        dma((tables,)),
-        dma((tables,)),
+        dma((2, tables)),
+        dma((2, tables)),
         dma((tables,)),
         dma((tables,)),
         dma((count,)),
         dma((count,)),
-        dma((count,)),
-        dma((count,)),
+        dma((count, state // ROWS)),
+        dma((count, state // ROWS)),
         dma((count,)),
         dma((count,)),
     ]
@@ -506,7 +560,14 @@
             flops=2 * 10**9, bytes_accessed=4 * 10**6, transcendentals=2 * 10**6
         ),
     )(*args)
-    return got[None]
+    return pl.pallas_call(
+        move,
+        out_shape=jax.ShapeDtypeStruct((1,) + got.shape, got.dtype),
+        in_specs=[pl.BlockSpec(memory_space=pl.ANY)],
+        out_specs=pl.BlockSpec(memory_space=pl.ANY),
+        scratch_shapes=[dma((4,))],
+        compiler_params=pltpu.CompilerParams(vmem_limit_bytes=63 * 2**20),
+    )(got)
 
 
 def solution(mesh):

time: 24.9 us -> 31.3 us (1.26)
  Pallas kernels: 23.1 us -> 31.2 us
  local copies, waits for them, and re-layouts: 1.67 us -> 0 us
    pallas_call x0 -> x1, Pallas kernels: none -> 9.08 us  [local(): pl.pallas_call(move, out_shape=jax.ShapeDtypeStruct((1,) + got.shape, got...]
    unnamed x1 -> x0, local copies, waits for them, and re-layouts: 1.67 us -> none
    pallas_call x1, Pallas kernels: 23.1 us -> 22.1 us  [local(): pl.pallas_call(functools.partial(kernel, tables, seqs), out_shape=jax.Sha...]
where the time goes in v3:
time: 31.3 us; the launch traced here: 31.2 us
  Pallas kernels  31.2 us (100%)
    pallas_call x1, Pallas kernels, local(): pl.pallas_call(functools.partial(kernel, tables, seqs), out_shape=jax.Sha...  22.1 us
    pallas_call x1, Pallas kernels, local(): pl.pallas_call(move, out_shape=jax.ShapeDtypeStruct((1,) + got.shape, got...  9.08 us

profile of v3, /device:TPU:25, one launch (start us, length us, event | category | flops | bytes accessed | tf_op | source)
XLA Modules:
  0.0 31.2 jit_solution(8177059002701735580)
XLA Ops:
  0.0 22.1 %shard_map.118.got = bf16[256,512]{1,0:T(8,128)(2,1)} custom-call(bf16[4,256,128]{2,1,0:T(8,128)(2,1)} %columns.1, f32[1,256]{1,0:T(1,128)} %gaps_h.1, f32[512]{0:T(512)} %norm_in_h.1, bf16[512,1024]{1,0:T(8,128)(2,1)} %w_gate_h.1, bf16[512,1280]{1,0:T(8,128)(2,1)} %w_xbc_h.1, bf16[16,512]{1,0:T(8,128)(2,1)} %bitcast.1, f32[16]{0:T(128)} %step_bias_h.1, ...), custom_call_target="tpu_custom_call" | custom-call | flops 2000000000 | bytes 4000000 | tf_op jit(solution)/shard_map/pallas_call | solution.py:550
  22.1 9.1 %shard_map.119 = bf16[1,256,512]{2,1,0:T(8,128)(2,1)} custom-call(bf16[256,512]{1,0:T(8,128)(2,1)} %shard_map.118.got), custom_call_target="tpu_custom_call" | custom-call | tf_op jit(solution)/shard_map/pallas_call | solution.py:563

commit v4 on v3

--- a/solution.py
+++ b/solution.py
@@ -78,6 +78,7 @@
     share_send,
     spread_s,
     nm,
+    mids,
     bias_row,
     out_row,
     load_sem,
@@ -205,8 +206,8 @@
     lane = lax.broadcasted_iota(jnp.int32, (heads, inner), 1) // head_dim
     head = lax.broadcasted_iota(jnp.int32, (heads, inner), 0)
     spread_s[...] = jnp.where(lane == head, 1.0, 0.0).astype(jnp.bfloat16)
-    before = lax.broadcasted_iota(jnp.int32, (length, length), 0)
-    after = lax.broadcasted_iota(jnp.int32, (length, length), 1)
+    before = lax.broadcasted_iota(jnp.int32, (q, q), 0)
+    after = lax.broadcasted_iota(jnp.int32, (q, q), 1)
     upper = jnp.where(before <= after, 1.0, 0.0).astype(jnp.bfloat16)
     keep = lax.broadcasted_iota(jnp.int32, (q, q), 0) >= lax.broadcasted_iota(
         jnp.int32, (q, q), 1
@@ -240,37 +241,58 @@
         for h in range(tables):
             rim(s, h, h).wait_recv()
 
-    norm(0, HALO + q)
-    project(0, HALO + q, slice(None))
-    for peer in peers:
-        across(1, peer, peer).wait_recv()
-    norm(HALO + q, HALO + length)
-
-    main = nm[HALO:, :]
-    step_raw = lax.dot_general(
-        w_step[...], main, (((1,), (1,)), ((), ())), preferred_element_type=jnp.float32
-    )
-    project(HALO + q, HALO + length, slice(inner, inner + 2 * state))
-    raw = step_raw + step_bias[...][:, None]
-    dt = jnp.maximum(raw, 0.0) + jnp.log1p(jnp.exp(-jnp.abs(raw)))
-    da = -rates[...][:, None] * dt * gaps[...]
-    d1 = da.astype(jnp.bfloat16)
-    left = da - d1.astype(jnp.float32)
-    d2, d3 = split(left)
-    cs = dot(d1, upper) + (dot(d2, upper) + dot(d3, upper))
-    last = cs[:, length - 1 : length]
-    cst = cs.T
-    faded = (jnp.exp(last - cs) * dt).T
-    closing = jnp.exp(cst[length - 16 :])
-
-    def conv(start, width):
+    def times(g):
+        here = nm[HALO + g * q : HALO + (g + 1) * q, :]
+        raw = lax.dot_general(
+            w_step[...], here, (((1,), (1,)), ((), ())), preferred_element_type=jnp.float32
+        )
+        raw = raw + step_bias[...][:, None]
+        dt = jnp.maximum(raw, 0.0) + jnp.log1p(jnp.exp(-jnp.abs(raw)))
+        da = -rates[...][:, None] * dt * gaps[:, g * q : (g + 1) * q]
+        d1 = da.astype(jnp.bfloat16)
+        d2, d3 = split(da - d1.astype(jnp.float32))
+        cs = dot(d1, upper) + (dot(d2, upper) + dot(d3, upper))
+        faded = (jnp.exp(cs[:, q - 1 : q] - cs) * dt).T
+        return dt, cs, faded
+
+    def conv(start, width, begin, count):
         lanes = pl.ds(start, width)
         total = bias_row[:, lanes]
         for k in range(taps):
             total = total + conv_weight[pl.ds(k, 1), lanes] * xb[
-                pl.ds(HALO - taps + 1 + k, length), lanes
+                pl.ds(HALO - taps + 1 + k + begin, count), lanes
             ]
         return silu(total)
+
+    def half_state(k, g, bt, faded):
+        start = k * CHUNK if g == 0 else pl.multiple_of(k * CHUNK, CHUNK)
+        x = conv(start, CHUNK, g * q, q).astype(jnp.bfloat16)
+        xs[k, g * q : (g + 1) * q, :] = x
+        weighted = expand(faded, pl.ds(start, CHUNK)) * x.astype(jnp.float32)
+        return dot(bt, weighted.astype(jnp.bfloat16))
+
+    norm(0, HALO + q)
+    project(0, HALO + q, slice(None))
+    dt0, cs0, faded0 = times(0)
+    bt0 = conv(inner, state, 0, q).T.astype(jnp.bfloat16)
+    for k in range(chunks):
+        states[k] = half_state(k, 0, bt0, faded0)
+
+    for peer in peers:
+        across(1, peer, peer).wait_recv()
+    norm(HALO + q, HALO + length)
+    dt1, cs1, faded1 = times(1)
+    project(HALO + q, HALO + length, slice(inner, inner + 2 * state))
+    bt1 = conv(inner, state, q, q).T.astype(jnp.bfloat16)
+    closed = cs0[:, q - 1 : q]
+    cs = jnp.concatenate([cs0, cs1 + closed], axis=1)
+    cst = cs.T
+    later = expand(jnp.exp(cs1.T[q - 16 :]), slice(None))[15:16]
+    ended = expand(jnp.exp(cst[length - 16 :]), slice(None))[15:16]
+    for k in range(chunks):
+        cut = slice(k * CHUNK, (k + 1) * CHUNK)
+        mids[k] = jnp.broadcast_to(later[:, cut], (8, CHUNK))
+        decays[k] = jnp.broadcast_to(ended[:, cut], (8, CHUNK))
 
     def to_partner(i):
         return pltpu.make_async_remote_copy(
@@ -283,28 +305,6 @@
         )
 
     rows = lax.broadcasted_iota(jnp.int32, (EXTRA, PIECE), 0)
-    bt = conv(inner, state).T.astype(jnp.bfloat16)
-    for j in range(chunks):
-        k = lax.rem(half * (1 - core) + j, chunks)
-        start = pl.multiple_of(k * CHUNK, CHUNK)
-        lanes = pl.ds(start, CHUNK)
-        project(HALO + q, HALO + length, lanes)
-        x = conv(start, CHUNK).astype(jnp.bfloat16)
-        xs[k] = x
-        weighted = expand(faded, lanes) * x.astype(jnp.float32)
-        made = dot(bt, weighted.astype(jnp.bfloat16))
-        decays[k] = jnp.broadcast_to(expand(closing, lanes)[15:16], (8, CHUNK))
-        if j >= half:
-            states[k] = made
-            continue
-        hi, lo = split(decays[k][0:1])
-        hi, lo = hi.astype(jnp.float32), lo.astype(jnp.float32)
-        for e in range(pieces):
-            cut = slice(e * PIECE, (e + 1) * PIECE)
-            tail = jnp.where(rows == 0, hi[:, cut], jnp.where(rows == 1, lo[:, cut], 0.0))
-            part_send[j * pieces + e, 0:state, :] = made[:, cut].astype(jnp.bfloat16)
-            part_send[j * pieces + e, state : state + EXTRA, :] = tail.astype(jnp.bfloat16)
-            to_partner(j * pieces + e).start()
 
     def chain(i, r):
         return pltpu.make_async_remote_copy(
@@ -378,12 +378,35 @@
             entering[place] = jnp.where(odd, between, came).astype(jnp.bfloat16)
         share(i, core).start()
 
-    @pl.when(pair == 0)
-    def _():
-        for i in range(half * pieces):
-            join(i)
-
-    cm = conv(inner + state, state).astype(jnp.bfloat16)
+    def first_join(j):
+        @pl.when(pair == 0)
+        def _():
+            for e in range(pieces):
+                join(j * pieces + e)
+
+    for j in range(half):
+        for mine in range(2):
+            k = half * (core if mine else 1 - core) + j
+            project(HALO + q, HALO + length, pl.ds(pl.multiple_of(k * CHUNK, CHUNK), CHUNK))
+            made = mids[k][0:1] * states[k] + half_state(k, 1, bt1, faded1)
+            if mine:
+                states[k] = made
+                continue
+            hi, lo = split(decays[k][0:1])
+            hi, lo = hi.astype(jnp.float32), lo.astype(jnp.float32)
+            for e in range(pieces):
+                cut = slice(e * PIECE, (e + 1) * PIECE)
+                tail = jnp.where(rows == 0, hi[:, cut], jnp.where(rows == 1, lo[:, cut], 0.0))
+                part_send[j * pieces + e, 0:state, :] = made[:, cut].astype(jnp.bfloat16)
+                part_send[j * pieces + e, state : state + EXTRA, :] = tail.astype(jnp.bfloat16)
+                to_partner(j * pieces + e).start()
+            if j > 0:
+                first_join(j - 1)
+    first_join(half - 1)
+
+    cm = conv(inner + state, state, 0, length).astype(jnp.bfloat16)
+    bt = jnp.concatenate([bt0, bt1], axis=1)
+    dt = jnp.concatenate([dt0, dt1], axis=1)
     cs2 = cs * LOG2E
     cs2t = cst * LOG2E
     row2 = jnp.where(dt > 0.0, cs2 - jnp.log(dt) * LOG2E, 3e38)
@@ -483,20 +506,6 @@
         for i in range(half * pieces):
             for r in range(parts):
                 chain(i, r).wait_send()
-
-
-def move(got, out, sem):
-    size = got.shape[0] // 4
-    copies = [
-        pltpu.make_async_copy(
-            got.at[pl.ds(i * size, size)], out.at[0, pl.ds(i * size, size)], sem.at[i]
-        )
-        for i in range(4)
-    ]
-    for copy in copies:
-        copy.start()
-    for copy in copies:
-        copy.wait()
 
 
 def local(tables, seqs, *args):
@@ -532,6 +541,7 @@
         pltpu.VMEM((count, state, PIECE), bf16),
         pltpu.VMEM((rates.shape[0], inner), bf16),
         pltpu.VMEM((HALO + length, w_gate.shape[0]), bf16),
+        pltpu.VMEM((chunks, 8, CHUNK), f32),
         pltpu.VMEM((1, w_xbc.shape[1]), f32),
         pltpu.VMEM((1, inner), f32),
         dma((11,)),
@@ -549,25 +559,18 @@
     ]
     got = pl.pallas_call(
         functools.partial(kernel, tables, seqs),
-        out_shape=jax.ShapeDtypeStruct((length, w_out.shape[1]), bf16),
+        out_shape=pltpu.VMEM((length, w_out.shape[1]), bf16),
         in_specs=[pl.BlockSpec(memory_space=pltpu.HBM)] * len(args),
         out_specs=pl.BlockSpec(memory_space=pltpu.VMEM),
         scratch_shapes=scratch,
         compiler_params=pltpu.CompilerParams(
-            collective_id=0, has_side_effects=True, vmem_limit_bytes=63 * 2**20
+            collective_id=0, has_side_effects=True, vmem_limit_bytes=60 * 10**6
         ),
         cost_estimate=pl.CostEstimate(
             flops=2 * 10**9, bytes_accessed=4 * 10**6, transcendentals=2 * 10**6
         ),
     )(*args)
-    return pl.pallas_call(
-        move,
-        out_shape=jax.ShapeDtypeStruct((1,) + got.shape, got.dtype),
-        in_specs=[pl.BlockSpec(memory_space=pl.ANY)],
-        out_specs=pl.BlockSpec(memory_space=pl.ANY),
-        scratch_shapes=[dma((4,))],
-        compiler_params=pltpu.CompilerParams(vmem_limit_bytes=63 * 2**20),
-    )(got)
+    return got[None]
 
 
 def solution(mesh):

time: 31.3 us -> 22.4 us (0.72)
  Pallas kernels: 31.2 us -> 21.6 us
  local copies, waits for them, and re-layouts: 0 us -> 0.71 us
    pallas_call x2 -> x1, Pallas kernels: 31.2 us -> 21.6 us  [local(): pl.pallas_call(functools.partial(kernel, tables, seqs), out_shape=pltpu.V...]
    unnamed x0 -> x1, local copies, waits for them, and re-layouts: none -> 0.71 us
where the time goes in v4:
time: 22.4 us; the launch traced here: 22.3 us
  Pallas kernels  21.6 us (96%)
  local copies, waits for them, and re-layouts  0.71 us (3%)
    pallas_call x1, Pallas kernels, local(): pl.pallas_call(functools.partial(kernel, tables, seqs), out_shape=pltpu.V...  21.6 us
    unnamed x1, local copies, waits for them, and re-layouts  0.71 us

profile of v4, /device:TPU:25, one launch (start us, length us, event | category | flops | bytes accessed | tf_op | source)
XLA Modules:
  0.0 22.3 jit_solution(9309671704472691257)
XLA Ops:
  0.0 21.6 %shard_map.118 = bf16[256,512]{1,0:T(8,128)(2,1)S(1)} custom-call(bf16[4,256,128]{2,1,0:T(8,128)(2,1)} %columns.1, f32[1,256]{1,0:T(1,128)} %gaps_h.1, f32[512]{0:T(512)} %norm_in_h.1, bf16[512,1024]{1,0:T(8,128)(2,1)} %w_gate_h.1, bf16[512,1280]{1,0:T(8,128)(2,1)} %w_xbc_h.1, bf16[16,512]{1,0:T(8,128)(2,1)} %bitcast.3, f32[16]{0:T(128)} %step_bias_h.1, ...), custom_call_target="tpu_custom_call" | custom-call | flops 2000000000 | bytes 4000000 | tf_op jit(solution)/shard_map/pallas_call | solution.py:560
  21.6 0.7 %copy.14 = bf16[1,256,512]{2,1,0:T(8,128)(2,1)} copy(bf16[1,256,512]{2,1,0:T(8,128)(2,1)S(1)} %bitcast.2) | data formatting | bytes 524288

commit v5 on v4

--- a/solution.py
+++ b/solution.py
@@ -129,25 +129,8 @@
 
     for off in range(1, tables):
         greet((s, lax.rem(t + off, tables)))
-    greet((partner, t))
-
-    @pl.when(s > 0)
-    def _():
-        for h in range(tables):
-            greet((s - 1, h))
-
-    @pl.when(s < seqs - 1)
-    def _():
-        for h in range(tables):
-            greet((s + 1, h))
-
-    @pl.when(pair > 0)
-    def _():
-        greet((s - 2, t))
-
-    @pl.when(pair < pairs - 1)
-    def _():
-        greet((s + 2, t))
+    for h in range(tables):
+        greet((partner, h))
 
     own.start()
     for load in loads:
@@ -161,12 +144,9 @@
     def count(held):
         return jnp.where(held, 1, 0)
 
+    earlier = count(pair > 0)
     pl.semaphore_wait(
-        barrier,
-        tables
-        + tables * (count(s > 0) + count(s < seqs - 1))
-        + count(pair > 0)
-        + count(pair < pairs - 1),
+        barrier, 2 * tables - 1 + earlier * (1 + tables * (1 - core))
     )
 
     q = length // 2
@@ -195,13 +175,31 @@
     for peer in peers:
         across(0, peer, t).start()
 
-    @pl.when(s < seqs - 1)
+    @pl.when(core == 0)
     def _():
         for h in range(tables):
             rim(s + 1, h, t).start()
 
     for peer in peers:
         across(1, peer, t).start()
+
+    @pl.when(pair < pairs - 1)
+    def _():
+        greet((s + 2, t))
+
+    @pl.when((pair < pairs - 1) & (core == 1))
+    def _():
+        for h in range(tables):
+            greet((s + 1, h))
+
+    @pl.when(pair > 0)
+    def _():
+        greet((s - 2, t))
+
+    @pl.when((pair > 0) & (core == 0))
+    def _():
+        for h in range(tables):
+            greet((s - 1, h))
 
     lane = lax.broadcasted_iota(jnp.int32, (heads, inner), 1) // head_dim
     head = lax.broadcasted_iota(jnp.int32, (heads, inner), 0)
@@ -217,6 +215,15 @@
     def expand(v, lanes):
         hi, lo = split(v)
         return dot(hi, spread_s[:, lanes]) + dot(lo, spread_s[:, lanes])
+
+    @pl.when(pair < pairs - 1)
+    def _():
+        pl.semaphore_wait(barrier, 1 + tables * core)
+
+    @pl.when((pair < pairs - 1) & (core == 1))
+    def _():
+        for h in range(tables):
+            rim(s + 1, h, t).start()
 
     for load in loads[:8]:
         load.wait()

time: 22.4 us -> 22.5 us (level)
  no operation moved by 1% of the time
where the time goes in v5:
time: 22.5 us; the launch traced here: 22.4 us
  Pallas kernels  21.7 us (96%)
  local copies, waits for them, and re-layouts  0.71 us (3%)
    pallas_call x1, Pallas kernels, local(): pl.pallas_call(functools.partial(kernel, tables, seqs), out_shape=pltpu.V...  21.7 us
    unnamed x1, local copies, waits for them, and re-layouts  0.71 us

profile of v5, /device:TPU:25, one launch (start us, length us, event | category | flops | bytes accessed | tf_op | source)
XLA Modules:
  0.0 22.4 jit_solution(3730789565527202620)
XLA Ops:
  0.0 21.7 %shard_map.118 = bf16[256,512]{1,0:T(8,128)(2,1)S(1)} custom-call(bf16[4,256,128]{2,1,0:T(8,128)(2,1)} %columns.1, f32[1,256]{1,0:T(1,128)} %gaps_h.1, f32[512]{0:T(512)} %norm_in_h.1, bf16[512,1024]{1,0:T(8,128)(2,1)} %w_gate_h.1, bf16[512,1280]{1,0:T(8,128)(2,1)} %w_xbc_h.1, bf16[16,512]{1,0:T(8,128)(2,1)} %bitcast.3, f32[16]{0:T(128)} %step_bias_h.1, ...), custom_call_target="tpu_custom_call" | custom-call | flops 2000000000 | bytes 4000000 | tf_op jit(solution)/shard_map/pallas_call | solution.py:567
  21.7 0.7 %copy.14 = bf16[1,256,512]{2,1,0:T(8,128)(2,1)} copy(bf16[1,256,512]{2,1,0:T(8,128)(2,1)S(1)} %bitcast.2) | data formatting | bytes 524288

commit v6 on v5

--- a/solution.py
+++ b/solution.py
@@ -79,6 +79,8 @@
     spread_s,
     nm,
     mids,
+    steep,
+    rise,
     bias_row,
     out_row,
     load_sem,
@@ -335,15 +337,23 @@
 
     odd = core == 1
 
+    def each(begin, count, act):
+        def one(i, carry):
+            act(i)
+            return carry
+
+        lax.fori_loop(begin, begin + count, one, 0)
+
+
     def join(i):
-        k, e = half * core + i // pieces, i % pieces
-        cut = slice(e * PIECE, (e + 1) * PIECE)
+        k = half * core + i // pieces
+        cut = pl.ds(pl.multiple_of(lax.rem(i, pieces) * PIECE, PIECE), PIECE)
         to_partner(i).wait_recv()
         theirs = part_recv[i, 0:state, :].astype(jnp.float32)
         tail = part_recv[i, state : state + EXTRA, :].astype(jnp.float32)
         their_decay = tail[0:1] + tail[1:2]
-        mine = states[k][:, cut]
-        my_decay = decays[k][0:1, cut]
+        mine = states[k, :, cut]
+        my_decay = decays[k, 0:1, cut]
         first = jnp.where(odd, theirs, mine)
         second = jnp.where(odd, mine, theirs)
         first_decay = jnp.where(odd, their_decay, my_decay)
@@ -388,8 +398,7 @@
     def first_join(j):
         @pl.when(pair == 0)
         def _():
-            for e in range(pieces):
-                join(j * pieces + e)
+            each(j * pieces, pieces, join)
 
     for j in range(half):
         for mine in range(2):
@@ -417,48 +426,50 @@
     cs2 = cs * LOG2E
     cs2t = cst * LOG2E
     row2 = jnp.where(dt > 0.0, cs2 - jnp.log(dt) * LOG2E, 3e38)
+    for k in range(chunks):
+        steep[k] = cs2t[:, k * per : (k + 1) * per]
+        rise[k] = row2[k * per : (k + 1) * per, :]
     scores = dot(cm, bt)
     top = jnp.where(keep, scores[:q, :q], 0.0)
     side = scores[q:, :q]
     end = jnp.where(keep, scores[q:, q:], 0.0)
 
-    def mix_of(h):
-        c0, c1 = cs2t[:q, h : h + 1], cs2t[q:, h : h + 1]
-        r0, r1 = row2[h : h + 1, :q], row2[h : h + 1, q:]
+    def mix_of(columns_k, rows_k, h):
+        c0, c1 = columns_k[:q, h : h + 1], columns_k[q:, h : h + 1]
+        r0, r1 = rows_k[h : h + 1, :q], rows_k[h : h + 1, q:]
         m0 = jnp.where(keep, top * jnp.exp2(c0 - r0), 0.0).astype(jnp.bfloat16)
         m1 = (side * jnp.exp2(c1 - r0)).astype(jnp.bfloat16)
         m2 = jnp.where(keep, end * jnp.exp2(c1 - r1), 0.0).astype(jnp.bfloat16)
         return m0, jnp.concatenate([m1, m2], axis=1)
 
     def intra(k):
+        columns_k, rows_k = steep[k], rise[k]
         for p in range(per // 2):
             pairx = xs[k, :, p * 2 * head_dim : (p + 1) * 2 * head_dim]
             got = []
             for e in range(2):
-                m0, m1 = mix_of(k * per + 2 * p + e)
+                m0, m1 = mix_of(columns_k, rows_k, 2 * p + e)
                 got.append(jnp.concatenate([dot(m0, pairx[:q]), dot(m1, pairx)], axis=0))
             y_in[k, :, p * 2 * head_dim : (p + 1) * 2 * head_dim] = jnp.where(low, got[0], got[1])
 
-    for k in range(chunks):
+    def one_chunk(k, carry):
         intra(k)
-        if k == 0:
-
-            @pl.when(pair > 0)
-            def _():
-                for i in range(half * pieces):
-                    join(i)
-
-            @pl.when(pair == 0)
-            def _():
-                for i in range(half * pieces):
-                    step(i, False)
-
-        if k != 1 and k < chunks - 1:
-
-            @pl.when(pair == max(k, 1))
-            def _():
-                for i in range(half * pieces):
-                    step(i, True)
+
+        @pl.when((k == 0) & (pair > 0))
+        def _():
+            each(0, half * pieces, join)
+
+        @pl.when((k == 0) & (pair == 0))
+        def _():
+            each(0, half * pieces, lambda i: step(i, False))
+
+        @pl.when((k != 1) & (k < chunks - 1) & (pair == jnp.maximum(k, 1)))
+        def _():
+            each(0, half * pieces, lambda i: step(i, True))
+
+        return carry
+
+    lax.fori_loop(0, chunks, one_chunk, 0)
 
     grown = expand(jnp.exp(cst), slice(None))
     for k in range(chunks):
@@ -481,18 +492,19 @@
 
     square = jnp.zeros((length, 1), jnp.float32)
     total = jnp.zeros((length, out.shape[1]), jnp.float32)
-    for j in range(half):
-
-        @pl.when(pair >= chunks - 1)
+    def last_chunk(n, carry):
+        @pl.when((n < half) & (pair >= chunks - 1))
+        def _():
+            each(n * pieces, pieces, lambda i: step(i, True))
+
+        @pl.when(n >= half)
         def _():
             for e in range(pieces):
-                step(j * pieces + e, True)
-
-        square, total = finish(half * core + j, square, total)
-    for j in range(half):
-        for e in range(pieces):
-            share(j * pieces + e, 1 - core).wait_recv()
-        square, total = finish(half * (1 - core) + j, square, total)
+                share((n - half) * pieces + e, 1 - core).wait_recv()
+
+        return finish(lax.rem(half * core + n, chunks), *carry)
+
+    square, total = lax.fori_loop(0, chunks, last_chunk, (square, total))
     out[...] = (total * lax.rsqrt(square / inner + epsilon)).astype(out.dtype)
 
     for peer in peers:
@@ -523,6 +535,7 @@
     inner = w_gate.shape[1]
     state = (w_xbc.shape[1] - inner) // 2
     chunks = inner // CHUNK
+    per = rates.shape[0] // chunks
     count = chunks // 2 * (CHUNK // PIECE)
     f32, bf16 = jnp.float32, jnp.bfloat16
     dma = pltpu.SemaphoreType.DMA
@@ -549,6 +562,8 @@
         pltpu.VMEM((rates.shape[0], inner), bf16),
         pltpu.VMEM((HALO + length, w_gate.shape[0]), bf16),
         pltpu.VMEM((chunks, 8, CHUNK), f32),
+        pltpu.VMEM((chunks, length, per), f32),
+        pltpu.VMEM((chunks, per, length), f32),
         pltpu.VMEM((1, w_xbc.shape[1]), f32),
         pltpu.VMEM((1, inner), f32),
         dma((11,)),

time: 22.5 us -> 22.6 us (level)
  no operation moved by 1% of the time
where the time goes in v6:
time: 22.6 us; the launch traced here: 22.5 us
  Pallas kernels  21.8 us (96%)
  local copies, waits for them, and re-layouts  0.71 us (3%)
    pallas_call x1, Pallas kernels, local(): pl.pallas_call(functools.partial(kernel, tables, seqs), out_shape=pltpu.V...  21.8 us
    unnamed x1, local copies, waits for them, and re-layouts  0.71 us

profile of v6, /device:TPU:25, one launch (start us, length us, event | category | flops | bytes accessed | tf_op | source)
XLA Modules:
  0.0 22.5 jit_solution(17861704880844519614)
XLA Ops:
  0.0 21.8 %shard_map.118 = bf16[256,512]{1,0:T(8,128)(2,1)S(1)} custom-call(bf16[4,256,128]{2,1,0:T(8,128)(2,1)} %columns.1, f32[1,256]{1,0:T(1,128)} %gaps_h.1, f32[512]{0:T(512)} %norm_in_h.1, bf16[512,1024]{1,0:T(8,128)(2,1)} %w_gate_h.1, bf16[512,1280]{1,0:T(8,128)(2,1)} %w_xbc_h.1, bf16[16,512]{1,0:T(8,128)(2,1)} %bitcast.3, f32[16]{0:T(128)} %step_bias_h.1, ...), custom_call_target="tpu_custom_call" | custom-call | flops 2000000000 | bytes 4000000 | tf_op jit(solution)/shard_map/pallas_call | solution.py:582
  21.8 0.7 %copy.14 = bf16[1,256,512]{2,1,0:T(8,128)(2,1)} copy(bf16[1,256,512]{2,1,0:T(8,128)(2,1)S(1)} %bitcast.2) | data formatting | bytes 524288

commit v7 on v6

--- a/solution.py
+++ b/solution.py
@@ -371,28 +371,28 @@
         middle[i] = first
         first_decays[i] = jnp.broadcast_to(first_decay, (8, PIECE))
 
+    def forward(i):
+        for r in range(parts):
+            band = slice(r * ROWS, (r + 1) * ROWS)
+            chain(i, r).wait_recv()
+
+            @pl.when(pair < pairs - 1)
+            def _():
+                came = chain_recv[i, band, :].astype(jnp.float32)
+                leaving = pair_decay[i][0:1] * came + pair_state[i, band, :]
+                chain_send[i, band, :] = leaving.astype(jnp.bfloat16)
+                chain(i, r).start()
+
     def step(i, entry):
         place = core * half * pieces + i
         if entry:
-            for r in range(parts):
-                band = slice(r * ROWS, (r + 1) * ROWS)
-                chain(i, r).wait_recv()
-                came = chain_recv[i, band, :].astype(jnp.float32)
-
-                @pl.when(pair < pairs - 1)
-                def _():
-                    leaving = pair_decay[i][0:1] * came + pair_state[i, band, :]
-                    chain_send[i, band, :] = leaving.astype(jnp.bfloat16)
-                    chain(i, r).start()
-
-                between = first_decays[i][0:1] * came + middle[i, band, :]
-                share_send[i, band, :] = jnp.where(odd, came, between).astype(jnp.bfloat16)
-                entering[place, band, :] = jnp.where(odd, between, came).astype(jnp.bfloat16)
+            came = chain_recv[i].astype(jnp.float32)
+            between = first_decays[i][0:1] * came + middle[i]
         else:
             came = jnp.zeros((state, PIECE), jnp.float32)
             between = middle[i]
-            share_send[i] = jnp.where(odd, came, between).astype(jnp.bfloat16)
-            entering[place] = jnp.where(odd, between, came).astype(jnp.bfloat16)
+        share_send[i] = jnp.where(odd, came, between).astype(jnp.bfloat16)
+        entering[place] = jnp.where(odd, between, came).astype(jnp.bfloat16)
         share(i, core).start()
 
     def first_join(j):
@@ -465,6 +465,7 @@
 
         @pl.when((k != 1) & (k < chunks - 1) & (pair == jnp.maximum(k, 1)))
         def _():
+            each(0, half * pieces, forward)
             each(0, half * pieces, lambda i: step(i, True))
 
         return carry
@@ -492,19 +493,17 @@
 
     square = jnp.zeros((length, 1), jnp.float32)
     total = jnp.zeros((length, out.shape[1]), jnp.float32)
-    def last_chunk(n, carry):
-        @pl.when((n < half) & (pair >= chunks - 1))
-        def _():
-            each(n * pieces, pieces, lambda i: step(i, True))
-
-        @pl.when(n >= half)
-        def _():
+    for n in range(chunks):
+        if n < half:
+
+            @pl.when(pair >= chunks - 1)
+            def _():
+                each(n * pieces, pieces, lambda i: (forward(i), step(i, True)))
+
+        else:
             for e in range(pieces):
                 share((n - half) * pieces + e, 1 - core).wait_recv()
-
-        return finish(lax.rem(half * core + n, chunks), *carry)
-
-    square, total = lax.fori_loop(0, chunks, last_chunk, (square, total))
+        square, total = finish(lax.rem(half * core + n, chunks), square, total)
     out[...] = (total * lax.rsqrt(square / inner + epsilon)).astype(out.dtype)
 
     for peer in peers:

time: 22.6 us -> 22.6 us (level)
  no operation moved by 1% of the time
where the time goes in v7:
time: 22.6 us; the launch traced here: 22.4 us
  Pallas kernels  21.7 us (96%)
  local copies, waits for them, and re-layouts  0.71 us (3%)
    pallas_call x1, Pallas kernels, local(): pl.pallas_call(functools.partial(kernel, tables, seqs), out_shape=pltpu.V...  21.7 us
    unnamed x1, local copies, waits for them, and re-layouts  0.71 us

profile of v7, /device:TPU:25, one launch (start us, length us, event | category | flops | bytes accessed | tf_op | source)
XLA Modules:
  0.0 22.4 jit_solution(10269657728834183371)
XLA Ops:
  0.0 21.7 %shard_map.118 = bf16[256,512]{1,0:T(8,128)(2,1)S(1)} custom-call(bf16[4,256,128]{2,1,0:T(8,128)(2,1)} %columns.1, f32[1,256]{1,0:T(1,128)} %gaps_h.1, f32[512]{0:T(512)} %norm_in_h.1, bf16[512,1024]{1,0:T(8,128)(2,1)} %w_gate_h.1, bf16[512,1280]{1,0:T(8,128)(2,1)} %w_xbc_h.1, bf16[16,512]{1,0:T(8,128)(2,1)} %bitcast.3, f32[16]{0:T(128)} %step_bias_h.1, ...), custom_call_target="tpu_custom_call" | custom-call | flops 2000000000 | bytes 4000000 | tf_op jit(solution)/shard_map/pallas_call | solution.py:581
  21.7 0.7 %copy.14 = bf16[1,256,512]{2,1,0:T(8,128)(2,1)} copy(bf16[1,256,512]{2,1,0:T(8,128)(2,1)S(1)} %bitcast.2) | data formatting | bytes 524288
